TPU v7x, 128 devices: a whole 4x4x4 slice. The times are simulated.
128 devices in a mesh: group: 16 (over z, y), cell: 8 (over x, core).
Axes of the slice: x: 4, y: 4, z: 4, core: 2. Of those that a mesh axis runs over, the one named last changes fastest.
Arguments:
- rest_shape: bfloat16 [3, 8192, 512], P(None, ('group', 'cell')), may hold values from -3 to 3
- state_start: float32 [12, 8192], P(None, ('group', 'cell')), may hold values from -3 to 3
- state_pred: float32 [12, 8192], P(None, ('group', 'cell')), may hold values from -3 to 3
- body_mass: float32 [8192], P(('group', 'cell')), may hold values from 0.5 to 4
- pair_body: int32 [786432], P(('group', 'cell')), may hold values from 0 to 63
- pair_vertex: int32 [786432], P(('group', 'cell')), may hold values from 0 to 511
- far_body: int32 [786432], P(('group', 'cell')), may hold values from 0 to 511
- far_vertex: int32 [786432], P(('group', 'cell')), may hold values from 0 to 511
- counts: int32 [128, 128], P(('group', 'cell')), may hold values from 0 to 48, as said below
Outputs:
- state_end: float32 [12, 8192], P(None, ('group', 'cell'))
Inputs may be any that keep to these rules, and one draw needn't show every extreme that they name: `counts`: entries of a row vary with the receiving device: a receiver's live slots from each sender lie between one and two eighths of 48 times a level of 1 to 4 drawn for that receiver; at least one entry equals 48.
All inputs are finite; a program needn't handle non-finite values.
Results may differ from a plain program's by a relative error of at most 0.00085.
Values may be sent and summed in bfloat16 or wider, within the bound.
A program may use at most 192 MiB of HBM per device.

v0:
```python
import math

import jax
import jax.numpy as jnp
from jax import lax
from jax.sharding import PartitionSpec as P

NEWTON = 2


KC0 = 40.0
KAPPA = 2.0
HIGH = lax.Precision.HIGHEST


def world_points(state, points):
    return (
        state[0:3] + points[0:1] * state[3:6] + points[1:2] * state[6:9] + points[2:3] * state[9:12]
    )


def inertia_blocks(rest_full, body_mass):
    verts = rest_full.shape[2]
    lever = jnp.concatenate([jnp.ones((1,) + rest_full.shape[1:], jnp.float32), rest_full], 0)
    moment = jnp.einsum("mbv,nbv->bmn", lever, lever, precision=HIGH) / verts
    moment = moment * body_mass[:, None, None]
    identity = jnp.eye(3, dtype=jnp.float32)
    return jnp.einsum("bmn,ik->bmink", moment, identity).reshape(moment.shape[0], 12, 12)


def row_features(near_rest, offset, alive, barrier):
    width = offset.shape[1]
    square = jnp.sum(offset * offset, 0)
    inverse = 1.0 / (square + 1.0)
    grad_coef = -2.0 * barrier * inverse * inverse * alive
    weight_one = 2.0 * barrier * inverse * inverse * alive
    root_two = jnp.sqrt(8.0 * barrier * inverse * inverse * inverse * alive)
    lever = jnp.concatenate([jnp.ones((1, width), jnp.float32), near_rest], 0)
    grad_rows = (lever[:, None, :] * (grad_coef * offset)[None]).reshape(12, width)
    moment_rows = (lever[:, None, :] * lever[None, :, :] * weight_one).reshape(16, width)
    vector_rows = (lever[:, None, :] * (root_two * offset)[None]).reshape(12, width)
    outer_rows = (vector_rows[:, None, :] * vector_rows[None, :, :]).reshape(144, width)
    return jnp.concatenate([grad_rows, moment_rows, outer_rows], 0)


def cholesky_blocks(hessian):
    factor = [[None] * 12 for _ in range(12)]
    for col in range(12):
        running = hessian[:, col, col]
        for inner in range(col):
            running = running - factor[col][inner] * factor[col][inner]
        pivot = jnp.sqrt(running)
        factor[col][col] = pivot
        for row in range(col + 1, 12):
            value = hessian[:, row, col]
            for inner in range(col):
                value = value - factor[row][inner] * factor[col][inner]
            factor[row][col] = value / pivot
    return factor


def solve_blocks(factor, gradient):
    forward = []
    for row in range(12):
        running = gradient[:, row]
        for col in range(row):
            running = running - factor[row][col] * forward[col]
        forward.append(running / factor[row][row])
    backward = [None] * 12
    for row in reversed(range(12)):
        running = forward[row]
        for col in range(row + 1, 12):
            running = running - factor[col][row] * backward[col]
        backward[row] = running / factor[row][row]
    return jnp.stack(backward, 1)


def newton_update(state, state_pred, inertia, totals):
    bodies = state.shape[1]
    stiff = jnp.array([0, 0, 0, 1, 1, 1, 1, 1, 1, 1, 1, 1], jnp.float32)
    target = jnp.array([0, 0, 0, 1, 0, 0, 0, 1, 0, 0, 0, 1], jnp.float32)
    identity = jnp.eye(3, dtype=jnp.float32)
    contact_grad = totals[0:12].T
    moments = totals[12:28].T.reshape(bodies, 4, 4)
    outers = totals[28:172].T.reshape(bodies, 12, 12)
    contact_hess = jnp.einsum("bmn,ik->bmink", moments, identity).reshape(bodies, 12, 12) + outers
    offset = (state - state_pred).T
    gradient = (
        jnp.einsum("bkl,bl->bk", inertia, offset, precision=HIGH)
        + 2.0 * KAPPA * stiff * (state.T - target)
        + contact_grad
    )
    hessian = inertia + jnp.diag(2.0 * KAPPA * stiff)[None] + contact_hess
    factor = cholesky_blocks(hessian)
    return state - solve_blocks(factor, gradient).T


def contact_totals(state, rest_shape, pair_body, pair_vertex, far_x, live_rows, barrier):
    row_count = pair_body.shape[0]
    width = math.gcd(row_count, 8192)
    bodies = state.shape[1]

    def accumulate(totals, block_index):
        first_row = block_index * width
        near_body = lax.dynamic_slice_in_dim(pair_body, first_row, width)
        near_point = lax.dynamic_slice_in_dim(pair_vertex, first_row, width)
        alive = lax.dynamic_slice_in_dim(live_rows, first_row, width)
        far_block = lax.dynamic_slice_in_dim(far_x, first_row, width, 1)
        near_rest = rest_shape[:, near_body, near_point].astype(jnp.float32)
        near_x = world_points(state[:, near_body], near_rest)
        features = row_features(near_rest, near_x - far_block, alive, barrier)
        selector = (near_body[None, :] == lax.iota(jnp.int32, bodies)[:, None]).astype(jnp.float32)
        return (totals + jnp.dot(features, selector.T, precision=HIGH), None)

    totals, _ = lax.scan(
        accumulate,
        jnp.zeros((172, bodies), jnp.float32),
        jnp.arange(row_count // width, dtype=jnp.int32),
    )
    return totals


def on_device(
    rest_shape,
    state_start,
    state_pred,
    body_mass,
    pair_body,
    pair_vertex,
    far_body,
    far_vertex,
    counts,
):
    bodies = rest_shape.shape[1]
    row_count = pair_body.shape[0]
    devices = lax.axis_size("group") * lax.axis_size("cell")
    capacity = row_count // devices
    barrier = KC0 * bodies / row_count
    rest_full = rest_shape.astype(jnp.float32)
    inertia = inertia_blocks(rest_full, body_mass)
    live_rows = (
        (lax.iota(jnp.int32, capacity)[None, :] < counts[0][:, None])
        .astype(jnp.float32)
        .reshape(row_count)
    )
    group_rest = lax.all_gather(rest_shape, "cell", axis=1, tiled=True)
    state = state_start
    for newton_step in range(NEWTON):
        group_state = lax.all_gather(state, "cell", axis=1, tiled=True)
        far_x = world_points(
            group_state[:, far_body], group_rest[:, far_body, far_vertex].astype(jnp.float32)
        )
        near_far = lax.all_to_all(
            far_x.astype(jnp.bfloat16), ("group", "cell"), split_axis=1, concat_axis=1, tiled=True
        ).astype(far_x.dtype)
        totals = contact_totals(
            state, rest_shape, pair_body, pair_vertex, near_far, live_rows, barrier
        )
        state = newton_update(state, state_pred, inertia, totals)
    return state


def solution(mesh):
    return jax.shard_map(
        on_device,
        mesh=mesh,
        in_specs=(
            P(None, ("group", "cell"), None),
            P(None, ("group", "cell")),
            P(None, ("group", "cell")),
            P(("group", "cell")),
            P(("group", "cell")),
            P(("group", "cell")),
            P(("group", "cell")),
            P(("group", "cell")),
            P(("group", "cell"), None),
        ),
        out_specs=P(None, ("group", "cell")),
        check_vma=False,
    )
```

profile of v0, /device:TPU:1, one launch (start us, length us, event | category | flops | bytes accessed | tf_op | source)
XLA Modules:
  0.0 461.5 jit_solution(1656171585242365037)
XLA Ops:
  9.1 14.6 %all-gather = f32[8,64,12]{1,2,0:T(8,128)S(1)} all-gather(f32[1,64,12]{1,2,0:T(8,128)} %bitcast.2106), channel_id=1, replica_groups=mesh['group'=16,'cell'=8] {'cell'}, dimensions={0}, use_global_device_ids=true | all-gather | bytes 27648 | tf_op jit(solution)/shard_map/all_gather | solution.py:149
  24.6 16.1 %gather_fusion.4 = f32[6144,12]{1,0:T(8,128)S(1)} fusion(f32[12,512]{0,1:T(8,128)S(1)} %bitcast.2100, s32[6144]{0:T(1024)S(1)} %get-tuple-element.703), kind=kCustom, calls=%fused_computation.4 | custom fusion | bytes 614400 | tf_op jit(solution)/shard_map/gather | solution.py:151
  43.2 42.4 %copy.165 = bf16[3,512,512]{0,2,1:T(8,128)(2,1)} copy(bf16[3,512,512]{2,1,0:T(8,128)(2,1)} %all-gather.4.cloned.1.call-done) | data formatting | bytes 3145728 | tf_op jit(solution)/shard_map/all_gather | solution.py:146
  85.6 71.6 %gather_fusion.5 = bf16[6144,3]{1,0:T(8,128)(2,1)S(1)} fusion(bf16[3,512,512]{0,2,1:T(8,128)(2,1)} %copy.165, s32[6144]{0:T(1024)S(1)} %get-tuple-element.702), kind=kCustom, calls=%fused_computation.5 | custom fusion | bytes 122880 | tf_op jit(solution)/shard_map/gather | solution.py:151
  163.2 9.6 %all-to-all-start = ((bf16[3,128,48]{2,0,1:T(4,128)(2,1)}), bf16[3,128,48]{2,0,1:T(4,128)(2,1)S(1)}, u32[]{:S(2)}, u32[]{:S(2)}) async-start(bf16[3,128,48]{2,0,1:T(4,128)(2,1)} %copy.166), calls=%async_computation | async-start | bytes 262144 | tf_op jit(solution)/shard_map/all_to_all | solution.py:153
  172.8 6.2 %copy.169 = bf16[3,64,512]{0,2,1:T(8,128)(2,1)} copy(bf16[3,64,512]{2,1,0:T(8,128)(2,1)S(1)} %copy-done) | data formatting | bytes 393216
  183.2 107.4 %while.22 = (s32[]{:T(128)}, f32[172,64]{0,1:T(8,128)S(1)}, s32[3]{0:T(128)S(1)}, s32[6144]{0:T(1024)S(1)}, s32[6144]{0:T(1024)}, /*index=5*/bf16[3,64,512]{0,2,...) while((s32[]{:T(128)}, f32[172,64]{0,1:T(8,128)S(1)}, ...), condition=%wide.region_2.3_spmd.clone, body=%wide.region_0.2_spmd.clone.sunk | while | flops 271926784 | bytes 7506137 | solution.py:115
  185.3 24.2 %gather_fusion.1 = bf16[2048,3]{1,0:T(8,128)(2,1)S(1)} fusion(bf16[3,64,512]{0,2,1:T(8,128)(2,1)} %get-tuple-element.905, s32[2048]{0:T(1024)S(1)} %get-tuple-element.836), kind=kCustom, calls=%fused_computation.clone.clone.1 | custom fusion | bytes 40960 | tf_op jit(solution)/shard_map/while/body/eval_jaxpr/gather | solution.py:109
  211.1 5.5 %gather_fusion = f32[2048,12]{1,0:T(8,128)S(1)} fusion(f32[12,64]{0,1:T(8,128)S(1)} %get-tuple-element.906, s32[2048]{0:T(1024)S(1)} %fusion.611), kind=kCustom, calls=%fused_computation.1.clone.clone.1 | custom fusion | bytes 204800 | tf_op jit(solution)/shard_map/while/body/eval_jaxpr/gather | solution.py:110
  221.1 24.3 %gather_fusion.1 = bf16[2048,3]{1,0:T(8,128)(2,1)S(1)} fusion(bf16[3,64,512]{0,2,1:T(8,128)(2,1)} %get-tuple-element.905, s32[2048]{0:T(1024)S(1)} %get-tuple-element.836), kind=kCustom, calls=%fused_computation.clone.clone.1 | custom fusion | bytes 40960 | tf_op jit(solution)/shard_map/while/body/eval_jaxpr/gather | solution.py:109
  246.9 5.5 %gather_fusion = f32[2048,12]{1,0:T(8,128)S(1)} fusion(f32[12,64]{0,1:T(8,128)S(1)} %get-tuple-element.906, s32[2048]{0:T(1024)S(1)} %fusion.611), kind=kCustom, calls=%fused_computation.1.clone.clone.1 | custom fusion | bytes 204800 | tf_op jit(solution)/shard_map/while/body/eval_jaxpr/gather | solution.py:110
  256.9 24.2 %gather_fusion.1 = bf16[2048,3]{1,0:T(8,128)(2,1)S(1)} fusion(bf16[3,64,512]{0,2,1:T(8,128)(2,1)} %get-tuple-element.905, s32[2048]{0:T(1024)S(1)} %get-tuple-element.836), kind=kCustom, calls=%fused_computation.clone.clone.1 | custom fusion | bytes 40960 | tf_op jit(solution)/shard_map/while/body/eval_jaxpr/gather | solution.py:109
  282.6 5.5 %gather_fusion = f32[2048,12]{1,0:T(8,128)S(1)} fusion(f32[12,64]{0,1:T(8,128)S(1)} %get-tuple-element.906, s32[2048]{0:T(1024)S(1)} %fusion.611), kind=kCustom, calls=%fused_computation.1.clone.clone.1 | custom fusion | bytes 204800 | tf_op jit(solution)/shard_map/while/body/eval_jaxpr/gather | solution.py:110
  292.9 12.7 %all-gather.1 = f32[8,64,12]{1,2,0:T(8,128)S(1)} all-gather(f32[1,64,12]{1,2,0:T(8,128)S(1)} %bitcast.2107), channel_id=1, replica_groups=mesh['group'=16,'cell'=8] {'cell'}, dimensions={0}, use_global_device_ids=true | all-gather | bytes 27648 | tf_op jit(solution)/shard_map/all_gather | solution.py:149
  305.8 19.0 %gather_fusion.6 = f32[6144,12]{1,0:T(8,128)S(1)} fusion(f32[12,512]{0,1:T(8,128)S(1)} %bitcast.2101, s32[6144]{0:T(1024)} %copy-done.5), kind=kCustom, calls=%fused_computation.6 | custom fusion | bytes 614400 | tf_op jit(solution)/shard_map/gather | solution.py:151
  329.0 5.9 %all-to-all-start.1 = ((bf16[3,128,48]{2,0,1:T(4,128)(2,1)}), bf16[3,128,48]{2,0,1:T(4,128)(2,1)S(1)}, u32[]{:S(2)}, u32[]{:S(2)}) async-start(bf16[3,128,48]{2,0,1:T(4,128)(2,1)} %copy.176), calls=%async_computation.1 | async-start | bytes 262144 | tf_op jit(solution)/shard_map/all_to_all | solution.py:153
  335.0 9.9 %all-to-all-done.1 = bf16[3,128,48]{2,0,1:T(4,128)(2,1)S(1)} async-done(((bf16[3,128,48]{2,0,1:T(4,128)(2,1)}), bf16[3,128,48]{2,0,1:T(4,128)(2,1)S(1)}, u32[]{:S(2)}, u32[]{:S(2)}) %all-to-all-start.1) | async-done | bytes 36896 | tf_op jit(solution)/shard_map/all_to_all | solution.py:153
  345.3 107.1 %while.23 = (s32[]{:T(128)}, f32[172,64]{0,1:T(8,128)S(1)}, s32[3]{0:T(128)S(1)}, s32[6144]{0:T(1024)S(1)}, s32[6144]{0:T(1024)}, /*index=5*/bf16[3,64,512]{0,2,...) while((s32[]{:T(128)}, f32[172,64]{0,1:T(8,128)S(1)}, ...), condition=%wide.region_5.6_spmd.clone, body=%wide.region_3.5_spmd.clone.sunk | while | flops 271926784 | bytes 7506137 | solution.py:115
  347.3 24.2 %gather_fusion.3 = bf16[2048,3]{1,0:T(8,128)(2,1)S(1)} fusion(bf16[3,64,512]{0,2,1:T(8,128)(2,1)} %get-tuple-element.947, s32[2048]{0:T(1024)S(1)} %get-tuple-element.859), kind=kCustom, calls=%fused_computation.2.clone.clone.1 | custom fusion | bytes 40960 | tf_op jit(solution)/shard_map/while/body/eval_jaxpr/gather | solution.py:109
  373.1 5.5 %gather_fusion.2 = f32[2048,12]{1,0:T(8,128)S(1)} fusion(f32[12,64]{0,1:T(8,128)S(1)} %get-tuple-element.948, s32[2048]{0:T(1024)S(1)} %fusion.616), kind=kCustom, calls=%fused_computation.3.clone.clone.1 | custom fusion | bytes 204800 | tf_op jit(solution)/shard_map/while/body/eval_jaxpr/gather | solution.py:110
  383.0 24.3 %gather_fusion.3 = bf16[2048,3]{1,0:T(8,128)(2,1)S(1)} fusion(bf16[3,64,512]{0,2,1:T(8,128)(2,1)} %get-tuple-element.947, s32[2048]{0:T(1024)S(1)} %get-tuple-element.859), kind=kCustom, calls=%fused_computation.2.clone.clone.1 | custom fusion | bytes 40960 | tf_op jit(solution)/shard_map/while/body/eval_jaxpr/gather | solution.py:109
  408.8 5.5 %gather_fusion.2 = f32[2048,12]{1,0:T(8,128)S(1)} fusion(f32[12,64]{0,1:T(8,128)S(1)} %get-tuple-element.948, s32[2048]{0:T(1024)S(1)} %fusion.616), kind=kCustom, calls=%fused_computation.3.clone.clone.1 | custom fusion | bytes 204800 | tf_op jit(solution)/shard_map/while/body/eval_jaxpr/gather | solution.py:110
  418.7 24.2 %gather_fusion.3 = bf16[2048,3]{1,0:T(8,128)(2,1)S(1)} fusion(bf16[3,64,512]{0,2,1:T(8,128)(2,1)} %get-tuple-element.947, s32[2048]{0:T(1024)S(1)} %get-tuple-element.859), kind=kCustom, calls=%fused_computation.2.clone.clone.1 | custom fusion | bytes 40960 | tf_op jit(solution)/shard_map/while/body/eval_jaxpr/gather | solution.py:109
  444.5 5.5 %gather_fusion.2 = f32[2048,12]{1,0:T(8,128)S(1)} fusion(f32[12,64]{0,1:T(8,128)S(1)} %get-tuple-element.948, s32[2048]{0:T(1024)S(1)} %fusion.616), kind=kCustom, calls=%fused_computation.3.clone.clone.1 | custom fusion | bytes 204800 | tf_op jit(solution)/shard_map/while/body/eval_jaxpr/gather | solution.py:110
  (269 shorter events, 56.1 us)
Async XLA Ops:
  6.5 36.7 %all-gather.4.cloned.1.call-start = ((), (), s32[]{:S(2)}) async-start(), calls=%async_computation.2 | async-start | bytes 1769472 | tf_op jit(solution)/shard_map/all_gather | solution.py:146
  24.6 61.0 %copy-start.5 = (s32[6144]{0:T(1024)}, s32[6144]{0:T(1024)S(1)}, u32[]{:S(2)}) copy-start(s32[6144]{0:T(1024)S(1)} %get-tuple-element.703) | copy-start | bytes 73732
  40.7 1.9 copy-start.30
  40.7 1.9 copy-start.24
  40.7 2.0 copy-start.12
  40.7 2.0 copy-start.20
  40.7 2.0 copy-start.29
  40.8 2.1 copy-start.3
  42.7 248.4 %copy-start.17 = (f32[12,12]{1,0:T(8,128)}, f32[12,12]{1,0:T(8,128)S(1)}, u32[]{:S(2)}) copy-start(f32[12,12]{1,0:T(8,128)S(1)} %fusion.62) | copy-start | bytes 1732
  157.4 4.8 %copy-start.1 = (f32[6144,12]{0,1:T(8,128)S(1)}, f32[6144,12]{0,1:T(8,128)}, u32[]{:S(2)}) copy-start(f32[6144,12]{0,1:T(8,128)} %copy.164) | copy-start | bytes 884740
  157.4 15.4 %copy-start = (bf16[3,64,512]{2,1,0:T(8,128)(2,1)S(1)}, bf16[3,64,512]{2,1,0:T(8,128)(2,1)}, u32[]{:S(2)}) copy-start(bf16[3,64,512]{2,1,0:T(8,128)(2,1)} %param.17) | copy-start | bytes 589828
  163.2 19.6 %all-to-all-start = ((bf16[3,128,48]{2,0,1:T(4,128)(2,1)}), bf16[3,128,48]{2,0,1:T(4,128)(2,1)S(1)}, u32[]{:S(2)}, u32[]{:S(2)}) async-start(bf16[3,128,48]{2,0,1:T(4,128)(2,1)} %copy.166), calls=%async_computation | async-start | bytes 262144 | tf_op jit(solution)/shard_map/all_to_all | solution.py:153
  172.8 118.0 %copy-start.22 = (f32[3,3]{1,0:T(4,128)}, f32[3,3]{1,0:T(4,128)S(1)}, u32[]{:S(2)}) copy-start(f32[3,3]{1,0:T(4,128)S(1)} %fusion.63) | copy-start | bytes 112
  172.8 10.4 %copy-start.2 = (s32[6144]{0:T(1024)S(1)}, s32[6144]{0:T(1024)}, u32[]{:S(2)}) copy-start(s32[6144]{0:T(1024)} %param.21) | copy-start | bytes 73732
  292.9 12.9 %copy-start.14 = (f32[12,64]{1,0:T(8,128)}, f32[12,64]{1,0:T(8,128)S(1)}, u32[]{:S(2)}) copy-start(f32[12,64]{1,0:T(8,128)S(1)} %get-tuple-element.456) | copy-start | bytes 9220
  324.8 1.9 copy-start.7
  324.8 1.9 copy-start.9
  324.8 1.9 copy-start.11
  324.9 10.0 %copy-start.19 = (f32[64,12]{0,1:T(8,128)S(1)}, f32[64,12]{0,1:T(8,128)}, u32[]{:S(2)}) copy-start(f32[64,12]{0,1:T(8,128)} %get-tuple-element.455) | copy-start | bytes 9220
  324.9 10.1 %copy-start.15 = (f32[12,64]{1,0:T(8,128)S(1)}, f32[12,64]{1,0:T(8,128)}, u32[]{:S(2)}) copy-start(f32[12,64]{1,0:T(8,128)} %copy-done.14) | copy-start | bytes 9220
  326.7 18.6 %copy-start.4 = (f32[172,64]{0,1:T(8,128)S(1)}, f32[172,64]{0,1:T(8,128)}, u32[]{:S(2)}) copy-start(f32[172,64]{0,1:T(8,128)} %custom-call.7) | copy-start | bytes 132100
  329.0 15.9 %all-to-all-start.1 = ((bf16[3,128,48]{2,0,1:T(4,128)(2,1)}), bf16[3,128,48]{2,0,1:T(4,128)(2,1)S(1)}, u32[]{:S(2)}, u32[]{:S(2)}) async-start(bf16[3,128,48]{2,0,1:T(4,128)(2,1)} %copy.176), calls=%async_computation.1 | async-start | bytes 262144 | tf_op jit(solution)/shard_map/all_to_all | solution.py:153
  345.3 107.3 %copy-start.23 = (f32[3,3]{1,0:T(4,128)S(1)}, f32[3,3]{1,0:T(4,128)}, u32[]{:S(2)}) copy-start(f32[3,3]{1,0:T(4,128)} %copy-done.22) | copy-start | bytes 112
  345.3 107.6 %copy-start.18 = (f32[12,12]{1,0:T(8,128)S(1)}, f32[12,12]{1,0:T(8,128)}, u32[]{:S(2)}) copy-start(f32[12,12]{1,0:T(8,128)} %copy-done.17) | copy-start | bytes 1732
  (10 other events, 10.2 us)
Sparse Core Ops, SparseCore 0:
  9.0 28.0 all-gather.3
where the time goes:
time: 468 us; the launch traced here: 462 us
  local copies, waits for them, and re-layouts  366 us (78%)
  blocking collectives  27.3 us (6%)
  starting transfers between devices  15.5 us (3%)
  between operations  14.2 us (3%)
  waiting for transfers between devices  14.1 us (3%)
  other arithmetic  12.8 us (3%)
  matrix products  6.65 us (1%)
  loops' own time  4.97 us (1%)
    gather x6, local copies, waits for them, and re-layouts, accumulate(): near_rest = rest_shape[:, near_body, near_point].astype(jnp.float32)  145 us
    gather x1, local copies, waits for them, and re-layouts, on_device(): group_rest[:, far_body, far_vertex].astype(jnp.float32)  71.6 us
    all_gather x1, local copies, waits for them, and re-layouts, on_device(): group_rest = lax.all_gather(rest_shape, 'cell', axis=1, tiled=True)  42.4 us
    gather x4, local copies, waits for them, and re-layouts, on_device(): group_state[:, far_body]  38.8 us
    gather x12, local copies, waits for them, and re-layouts, accumulate(): near_x = world_points(state[:, near_body], near_rest)  34.8 us
    all_gather x2, blocking collectives, on_device(): group_state = lax.all_gather(state, 'cell', axis=1, tiled=True)  27.3 us
    all_to_all x2, starting transfers between devices, on_device(): lax.all_to_all(far_x.astype(jnp.bfloat16), ('group', 'cell'), split_axis=...  15.5 us
    all_to_all x2, waiting for transfers between devices, on_device(): lax.all_to_all(far_x.astype(jnp.bfloat16), ('group', 'cell'), split_axis=...  13.3 us
  transfers between devices with their start and end apart: 3, of which 2 were waited for; matrix products, arithmetic and copies ran while one was open for 6% of the time, Pallas kernels for 0%

commit v1 on v0

v1 whole, which is shorter than its diff:
```python
import jax
import jax.numpy as jnp
from jax import lax
from jax.experimental import pallas as pl
from jax.experimental.pallas import tpu as pltpu
from jax.sharding import PartitionSpec as P

NEWTON = 2
KC0 = 40.0
KAPPA = 2.0
MESH = pl.DeviceIdType.MESH
F32 = jnp.float32
BF16 = jnp.bfloat16
I32 = jnp.int32

V = 512
B = 64
ROWS = 6144
CAP = 48
NG = 16
NC = 8
DENSE = (ROWS // 128, 128)
PER_G = ROWS // NG
W_NEAR = 512
W_FAR = 256
NT = (((1,), (1,)), ((), ()))

MN = [(m, n) for m in range(4) for n in range(m, 4)]
IK = [(i, k) for i in range(3) for k in range(i, 3)]


def iota(shape, dim):
    return lax.broadcasted_iota(I32, shape, dim)


def one_hot_vertex(vertex):
    width = vertex.shape[1]
    rows = (iota((V, width), 0) - V // 2).astype(BF16)
    mine = jnp.broadcast_to((vertex - V // 2).astype(BF16), (V, width))
    return jnp.where(rows == mine, jnp.ones((), BF16), jnp.zeros((), BF16))


def pick_bodies(acc, picked, body, blocks):
    for n in range(blocks):
        for bg in range(B // 8):
            mine = body == n * B + bg * 8
            for c in range(3):
                at = n * 3 * B + c * B + bg * 8
                acc[c] = jnp.where(mine, picked[at : at + 8], acc[c])
    return acc


def gather_lanes(row, index):
    return jnp.take_along_axis(
        jnp.broadcast_to(row, index.shape), index, axis=1, mode="promise_in_bounds"
    )


def solve(hess, grad):
    factor = [[None] * 12 for _ in range(12)]
    inv = [None] * 12
    for col in range(12):
        running = hess(col, col)
        for inner in range(col):
            running = running - factor[col][inner] * factor[col][inner]
        inv[col] = 1.0 / jnp.sqrt(running)
        for row in range(col + 1, 12):
            value = hess(row, col)
            for inner in range(col):
                value = value - factor[row][inner] * factor[col][inner]
            factor[row][col] = value * inv[col]
    forward = []
    for row in range(12):
        running = grad[row]
        for col in range(row):
            running = running - factor[row][col] * forward[col]
        forward.append(running * inv[row])
    backward = [None] * 12
    for row in reversed(range(12)):
        running = forward[row]
        for col in range(row + 1, 12):
            running = running - factor[col][row] * backward[col]
        backward[row] = running * inv[row]
    return backward


def kernel(
    rest_ref, state_ref, pred_ref, mass_ref, nb_ref, nv_ref, fb_ref, fv_ref, counts_ref,
    out_ref,
    restg, ksend, krecv, ssend, srecv, xsend, xrecv,
    oh, ohb, acc, keyd, vrow, brow, nbrow, nvrow, fbd, fr, nr, live, p16, q9, feat, tot, inert, xd,
    rest_ss, rest_rs, k_ss, k_rs, s_ss, s_rs, x_ss, x_rs,
):
    g = lax.axis_index("group")
    c = lax.axis_index("cell")
    kc = KC0 * B / ROWS

    def cell_peer(d):
        return lax.rem(c + d, NC)

    def group_peer(d):
        return lax.rem(g + d, NG)

    barrier = pltpu.get_barrier_semaphore()

    @pl.loop(1, NC)
    def _(d):
        pl.semaphore_signal(barrier, inc=1, device_id=(g, cell_peer(d)), device_id_type=MESH)

    @pl.loop(1, NG)
    def _(d):
        pl.semaphore_signal(barrier, inc=1, device_id=(group_peer(d), c), device_id_type=MESH)

    for t in range(3):
        rows = pl.ds(t, NG, stride=3)
        keyd[:, t * 128 : (t + 1) * 128] = fb_ref[rows, :] * V + fv_ref[rows, :]
    ksend[...] = jnp.zeros_like(ksend)
    for s in range(NC):
        ksend[s, :, 0:CAP] = keyd[:, s * CAP : (s + 1) * CAP]
    ssend[...] = jnp.zeros_like(ssend)
    ssend[0, 0:12, :] = jnp.concatenate([state_ref[...], state_ref[...]], axis=1)

    pl.semaphore_wait(barrier, NC - 1 + NG - 1)

    def key_copy(to, slot):
        return pltpu.make_async_remote_copy(
            ksend.at[to], krecv.at[slot], k_ss.at[to], k_rs.at[slot],
            device_id=(g, to), device_id_type=MESH,
        )

    def rest_copy(to, slot):
        return pltpu.make_async_remote_copy(
            rest_ref, restg.at[slot], rest_ss.at[to], rest_rs.at[slot],
            device_id=(g, to), device_id_type=MESH,
        )

    def state_copy(it, to, slot):
        return pltpu.make_async_remote_copy(
            ssend.at[it], srecv.at[it, slot], s_ss.at[it, to], s_rs.at[it, slot],
            device_id=(g, to), device_id_type=MESH,
        )

    def x_copy(it, to, slot):
        return pltpu.make_async_remote_copy(
            xsend.at[it, to], xrecv.at[it, slot], x_ss.at[it, to], x_rs.at[it, slot],
            device_id=(to, c), device_id_type=MESH,
        )

    @pl.loop(1, NC)
    def _(d):
        key_copy(cell_peer(d), c).start()

    @pl.loop(1, NC)
    def _(d):
        rest_copy(cell_peer(d), c).start()

    @pl.loop(1, NC)
    def _(d):
        state_copy(0, cell_peer(d), c).start()

    restg[c] = rest_ref[...]
    krecv[c] = ksend[c]
    srecv[0, c] = ssend[0]

    @pl.loop(0, DENSE[0])
    def _(j):
        lanes = pl.ds(pl.multiple_of(j * 128, 128), 128)
        nvrow[0:1, lanes] = nv_ref[pl.ds(j, 1), :]
        nbrow[0:1, lanes] = nb_ref[pl.ds(j, 1), :]

    p16[...] = jnp.zeros_like(p16)

    @pl.loop(0, ROWS // W_NEAR)
    def _(j):
        lanes = pl.ds(pl.multiple_of(j * W_NEAR, W_NEAR), W_NEAR)
        picked = jnp.dot(
            rest_ref[...], one_hot_vertex(nvrow[0:1, lanes]), preferred_element_type=F32
        )
        body = nbrow[0:1, lanes]
        ohb[:, lanes] = jnp.where(
            iota((B, W_NEAR), 0) == jnp.broadcast_to(body, (B, W_NEAR)), 1.0, 0.0
        ).astype(BF16)
        tile = jnp.broadcast_to(body, (8, W_NEAR)) - iota((8, W_NEAR), 0)
        found = pick_bodies([jnp.zeros((8, W_NEAR), F32)] * 3, picked, tile, 1)
        r = [jnp.sum(f, 0, keepdims=True) for f in found]
        lever = [jnp.ones((1, W_NEAR), F32)] + r
        for f, (m, n) in enumerate(MN):
            p16[f : f + 1, lanes] = lever[m] * lever[n]
        for i in range(3):
            for t in range(W_NEAR // 128):
                nr[i, pl.ds(j * (W_NEAR // 128) + t, 1), :] = r[i][:, t * 128 : (t + 1) * 128]

    row = iota(DENSE, 0) * 128 + iota(DENSE, 1)
    sender = (row * 43691) >> 21
    count = gather_lanes(counts_ref[...], sender)
    live[...] = jnp.where(row - sender * CAP < count, 1.0, 0.0)

    ones = jnp.ones((8, V), BF16)
    body_rest = [rest_ref[i * B : (i + 1) * B, :] for i in range(3)]
    scale = mass_ref[...] * (1.0 / V)
    inert[0:1, :] = mass_ref[...]
    for f, (m, n) in enumerate(MN):
        if n == 0:
            continue
        if m == 0:
            total = lax.dot_general(ones, body_rest[n - 1], NT, preferred_element_type=F32)
        else:
            product = body_rest[m - 1].astype(F32) * body_rest[n - 1].astype(F32)
            high = product.astype(BF16)
            low = (product - high.astype(F32)).astype(BF16)
            total = lax.dot_general(ones, high, NT, preferred_element_type=F32)
            total = total + lax.dot_general(ones, low, NT, preferred_element_type=F32)
        inert[f : f + 1, :] = total[0:1] * scale

    @pl.loop(1, NC)
    def _(d):
        key_copy(c, cell_peer(d)).wait_recv()

    for s in range(NC):
        keyd[:, s * CAP : (s + 1) * CAP] = krecv[s, :, 0:CAP]
    for t in range(3):
        fbd[pl.ds(t, NG, stride=3), :] = keyd[:, t * 128 : (t + 1) * 128] >> 9

    @pl.loop(0, NG)
    def _(j):
        lanes = pl.ds(pl.multiple_of(j * PER_G, 128), PER_G)
        key = keyd[pl.ds(j, 1), :]
        vrow[0:1, lanes] = key & (V - 1)
        brow[0:1, lanes] = key >> 9

    @pl.loop(0, ROWS // W_NEAR)
    def _(j):
        lanes = pl.ds(pl.multiple_of(j * W_NEAR, W_NEAR), W_NEAR)
        oh[:, lanes] = one_hot_vertex(vrow[0:1, lanes])

    acc[...] = jnp.zeros_like(acc)
    x = lax.div(c, 2)
    for step, d in enumerate((0, 1, 3, 2)):
        chip = lax.rem(x + d, NC // 2)
        if step == 0:
            rest_copy(c, c + 1 - 2 * lax.rem(c, 2)).wait_recv()
        else:
            for k in range(2):
                rest_copy(c, chip * 2 + k).wait_recv()

        def look(j, carry, chip=chip):
            lanes = pl.ds(pl.multiple_of(j * W_FAR, W_FAR), W_FAR)
            table = restg[pl.ds(chip * 2, 2)].reshape(2 * 3 * B, V)
            picked = jnp.dot(table, oh[:, lanes], preferred_element_type=F32)
            body = jnp.broadcast_to(brow[0:1, lanes] - chip * 2 * B, (8, W_FAR))
            found = [acc[i * 8 : i * 8 + 8, lanes] for i in range(3)]
            found = pick_bodies(found, picked, body - iota((8, W_FAR), 0), 2)
            for i in range(3):
                acc[i * 8 : i * 8 + 8, lanes] = found[i]
            return carry

        lax.fori_loop(0, ROWS // W_FAR, look, 0, unroll=4)

    @pl.loop(0, DENSE[0])
    def _(j):
        lanes = pl.ds(pl.multiple_of(j * 128, 128), 128)
        for i in range(3):
            fr[i, pl.ds(j, 1), :] = jnp.sum(acc[i * 8 : i * 8 + 8, lanes], 0, keepdims=True)

    state = [state_ref[e : e + 1, :] for e in range(12)]
    for it in range(NEWTON):
        @pl.loop(1, NC)
        def _(d, it=it):
            state_copy(it, c, cell_peer(d)).wait_recv()

        pick = iota((16, 128), 1) < B
        low = fbd[...] & 127
        chip_of = fbd[...] >> 7
        far = [None] * 12
        for chip in range(NC // 2):
            table = jnp.where(pick, srecv[it, 2 * chip], srecv[it, 2 * chip + 1])
            here = chip_of == chip
            for e in range(12):
                value = gather_lanes(table[e : e + 1], low)
                far[e] = value if chip == 0 else jnp.where(here, value, far[e])
        for i in range(3):
            xd[i] = far[i] + fr[0] * far[3 + i] + fr[1] * far[6 + i] + fr[2] * far[9 + i]

        @pl.loop(0, NG)
        def _(j, it=it):
            for i in range(3):
                for t in range(3):
                    at = i * PER_G + t * 128
                    xsend[it, j, :, at : at + 128] = xd[i, pl.ds(j * 3 + t, 1), :]

        @pl.loop(1, NG)
        def _(d, it=it):
            x_copy(it, group_peer(d), g).start()

        xrecv[it, g] = xsend[it, g]

        near_index = nb_ref[...]
        near = [gather_lanes(jnp.concatenate([s, s], axis=1), near_index) for s in state]
        near_x = [
            near[i] + nr[0] * near[3 + i] + nr[1] * near[6 + i] + nr[2] * near[9 + i]
            for i in range(3)
        ]

        @pl.loop(1, NG)
        def _(d, it=it):
            x_copy(it, g, group_peer(d)).wait_recv()

        @pl.loop(0, NG)
        def _(j, it=it):
            for i in range(3):
                for t in range(3):
                    at = i * PER_G + t * 128
                    xd[i, pl.ds(j * 3 + t, 1), :] = xrecv[it, j, :, at : at + 128]

        off = [near_x[i] - xd[i] for i in range(3)]
        w = 1.0 / (off[0] * off[0] + off[1] * off[1] + off[2] * off[2] + 1.0)
        h1 = (2.0 * kc) * w * w * live[...]
        h2 = 4.0 * h1 * w
        for f, (i, k) in enumerate(IK):
            value = h2 * off[i] * off[k]
            q9[f] = value + h1 if i == k else value
        for i in range(3):
            q9[6 + i] = -h1 * off[i]

        def features(j, carry):
            lanes = pl.ds(pl.multiple_of(j * 128, 128), 128)
            lever = p16[:, lanes]
            for f in range(6):
                value = lever * q9[f, pl.ds(j, 1), :]
                high = value.astype(BF16)
                feat[f * 16 : f * 16 + 16, lanes] = high
                feat[128 + f * 16 : 128 + f * 16 + 16, lanes] = (value - high.astype(F32)).astype(
                    BF16
                )
            for f, pair in enumerate(((6, 7), (8, 8))):
                value = jnp.concatenate(
                    [lever[0:8] * q9[q, pl.ds(j, 1), :] for q in pair], axis=0
                )
                high = value.astype(BF16)
                at = 96 + f * 16
                feat[at : at + 16, lanes] = high
                feat[128 + at : 128 + at + 16, lanes] = (value - high.astype(F32)).astype(BF16)
            return carry

        lax.fori_loop(0, DENSE[0], features, 0, unroll=2)
        both = lax.dot_general(feat[...], ohb[...], NT, preferred_element_type=F32)
        tot[...] = both[0:128] + both[128:256]

        def moment(m, n):
            f = MN.index((min(m, n), max(m, n)))
            return inert[f : f + 1, :]

        def hess(a, b):
            (m, i), (n, k) = divmod(a, 3), divmod(b, 3)
            f = IK.index((min(i, k), max(i, k))) * 16 + MN.index((min(m, n), max(m, n)))
            value = tot[f : f + 1, :]
            if i == k:
                value = value + moment(m, n)
            if a == b and m > 0:
                value = value + 2.0 * KAPPA
            return value

        shift = [state[e] - pred_ref[e : e + 1, :] for e in range(12)]
        grad = []
        for e in range(12):
            m, i = divmod(e, 3)
            at = 96 + i * 8 + m
            value = tot[at : at + 1, :]
            for n in range(4):
                value = value + moment(m, n) * shift[3 * n + i]
            if m > 0:
                value = value + 2.0 * KAPPA * (state[e] - (1.0 if m - 1 == i else 0.0))
            grad.append(value)
        step = solve(hess, grad)
        state = [state[e] - step[e] for e in range(12)]
        if it + 1 < NEWTON:
            for e in range(12):
                ssend[it + 1, e : e + 1, :] = jnp.concatenate([state[e], state[e]], axis=1)

            @pl.loop(1, NC)
            def _(d, it=it):
                state_copy(it + 1, cell_peer(d), c).start()

            srecv[it + 1, c] = ssend[it + 1]
        else:
            for e in range(12):
                out_ref[e : e + 1, :] = state[e]

    @pl.loop(1, NC)
    def _(d):
        key_copy(cell_peer(d), c).wait_send()
        rest_copy(cell_peer(d), c).wait_send()
        for it in range(NEWTON):
            state_copy(it, cell_peer(d), c).wait_send()

    @pl.loop(1, NG)
    def _(d):
        for it in range(NEWTON):
            x_copy(it, group_peer(d), g).wait_send()


def on_device(rest, state, pred, mass, pair_body, pair_vertex, far_body, far_vertex, counts):
    dma = pltpu.SemaphoreType.DMA
    vmem = pltpu.VMEM
    return pl.pallas_call(
        kernel,
        out_shape=jax.ShapeDtypeStruct((12, B), F32),
        in_specs=[pl.BlockSpec(memory_space=vmem)] * 9,
        out_specs=pl.BlockSpec(memory_space=vmem),
        scratch_shapes=[
            vmem((NC, 3 * B, V), BF16),
            vmem((NC, NG, 128), I32),
            vmem((NC, NG, 128), I32),
            vmem((NEWTON, 16, 128), F32),
            vmem((NEWTON, NC, 16, 128), F32),
            vmem((NEWTON, NG, 1, 3 * PER_G), F32),
            vmem((NEWTON, NG, 1, 3 * PER_G), F32),
            vmem((V, ROWS), BF16),
            vmem((B, ROWS), BF16),
            vmem((24, ROWS), F32),
            vmem((NG, PER_G), I32),
            vmem((1, ROWS), I32),
            vmem((1, ROWS), I32),
            vmem((1, ROWS), I32),
            vmem((1, ROWS), I32),
            vmem(DENSE, I32),
            vmem((3,) + DENSE, F32),
            vmem((3,) + DENSE, F32),
            vmem(DENSE, F32),
            vmem((16, ROWS), F32),
            vmem((9,) + DENSE, F32),
            vmem((256, ROWS), BF16),
            vmem((128, B), F32),
            vmem((16, B), F32),
            vmem((3,) + DENSE, F32),
            dma((NC,)),
            dma((NC,)),
            dma((NC,)),
            dma((NC,)),
            dma((NEWTON, NC)),
            dma((NEWTON, NC)),
            dma((NEWTON, NG)),
            dma((NEWTON, NG)),
        ],
        compiler_params=pltpu.CompilerParams(
            collective_id=0, has_side_effects=True, vmem_limit_bytes=48 * 2**20
        ),
    )(
        rest.reshape(3 * B, V),
        state,
        pred,
        mass.reshape(1, B),
        pair_body.reshape(DENSE),
        pair_vertex.reshape(DENSE),
        far_body.reshape(DENSE),
        far_vertex.reshape(DENSE),
        counts,
    )


def solution(mesh):
    both = ("group", "cell")
    return jax.shard_map(
        on_device,
        mesh=mesh,
        in_specs=(
            P(None, both, None),
            P(None, both),
            P(None, both),
            P(both),
            P(both),
            P(both),
            P(both),
            P(both),
            P(both, None),
        ),
        out_specs=P(None, both),
        check_vma=False,
    )
```

time: 468 us -> 66.8 us (0.14); the launches traced: 462 us -> 66.3 us
  local copies, waits for them, and re-layouts: 366 us -> 5.87 us
  Pallas kernels: 0 us -> 60.4 us
  blocking collectives: 27.3 us -> 0 us
  starting transfers between devices: 15.5 us -> 0 us
  between operations: 14.2 us -> 0.02 us
  waiting for transfers between devices: 14.1 us -> 0 us
  other arithmetic: 12.8 us -> 0 us
  matrix products: 6.65 us -> 0 us
  loops' own time: 4.97 us -> 0 us
    gather x23 -> x0, local copies, waits for them, and re-layouts: 291 us -> none  [the longest x6 145 us: accumulate(): near_rest = rest_shape[:, near_body, near_point].astype(jnp.float32)]
    pallas_call x0 -> x1, Pallas kernels: none -> 60.4 us  [on_device(): pl.pallas_call(kernel, out_shape=jax.ShapeDtypeStruct((12, B), F32), in_s...]
    all_gather x3 -> x0, local copies, waits for them, and re-layouts: 42.7 us -> none  [the longest x1 42.4 us: on_device(): group_rest = lax.all_gather(rest_shape, 'cell', axis=1, tiled=True)]
    all_gather x2 -> x0, blocking collectives: 27.3 us -> none  [on_device(): group_state = lax.all_gather(state, 'cell', axis=1, tiled=True)]
    all_to_all x2 -> x0, starting transfers between devices: 15.5 us -> none  [on_device(): lax.all_to_all(far_x.astype(jnp.bfloat16), ('group', 'cell'), split_axis=...]
    all_to_all x2 -> x0, waiting for transfers between devices: 13.3 us -> none  [on_device(): lax.all_to_all(far_x.astype(jnp.bfloat16), ('group', 'cell'), split_axis=...]
    slice x9 -> x0, local copies, waits for them, and re-layouts: 12.8 us -> none  [the longest x7 12.8 us: world_points(): points[0:1] * state[3:6]]
    dot_general x7 -> x0, matrix products: 6.65 us -> none  [the longest x6 6.26 us: accumulate(): return (totals + jnp.dot(features, selector.T, precision=HIGH), None)]
  transfers between devices with their start and end apart: 3 -> 0, of which waited for: 2 -> 0; matrix products, arithmetic and copies ran while one was open for 6% -> 0% of each run, Pallas kernels for 0% -> 0%
where the time goes in v1:
time: 66.8 us; the launch traced here: 66.3 us
  Pallas kernels  60.4 us (90%)
  local copies, waits for them, and re-layouts  5.87 us (9%)
    pallas_call x1, Pallas kernels, on_device(): pl.pallas_call(kernel, out_shape=jax.ShapeDtypeStruct((12, B), F32), in_s...  60.4 us
    unnamed x19, local copies, waits for them, and re-layouts  5.87 us

profile of v1, /device:TPU:1, one launch (start us, length us, event | category | flops | bytes accessed | tf_op | source)
XLA Modules:
  0.0 66.3 jit_solution(6857223749499890695)
XLA Ops:
  0.0 0.0 copy-start.5
  0.0 0.0 copy-start.7
  0.0 0.0 copy-start.8
  0.0 0.7 %copy-done.5 = f32[12,64]{1,0:T(8,128)S(1)} copy-done((f32[12,64]{1,0:T(8,128)S(1)}, f32[12,64]{1,0:T(8,128)}, u32[]{:S(2)}) %copy-start.5) | copy-done | bytes 3096
  0.7 0.0 copy-done.7
  0.7 0.0 copy-done.8
  0.7 0.0 copy-start
  0.7 0.9 %copy-done = bf16[3,64,512]{2,1,0:T(8,128)(2,1)S(1)} copy-done((bf16[3,64,512]{2,1,0:T(8,128)(2,1)S(1)}, bf16[3,64,512]{2,1,0:T(8,128)(2,1)}, u32[]{:S(2)}) %copy-start) | copy-done | bytes 196632
  1.6 0.0 copy-start.1
  1.6 0.7 %copy-done.1 = s32[6144]{0:T(1024)S(1)} copy-done((s32[6144]{0:T(1024)S(1)}, s32[6144]{0:T(1024)}, u32[]{:S(2)}) %copy-start.1) | copy-done | bytes 24600
  2.4 0.0 copy-start.2
  2.4 0.7 %copy-done.2 = s32[6144]{0:T(1024)S(1)} copy-done((s32[6144]{0:T(1024)S(1)}, s32[6144]{0:T(1024)}, u32[]{:S(2)}) %copy-start.2) | copy-done | bytes 24600
  3.1 0.0 copy-start.3
  3.1 0.7 %copy-done.3 = s32[6144]{0:T(1024)S(1)} copy-done((s32[6144]{0:T(1024)S(1)}, s32[6144]{0:T(1024)}, u32[]{:S(2)}) %copy-start.3) | copy-done | bytes 24600
  3.8 0.0 copy-start.4
  3.8 0.7 %copy-done.4 = s32[6144]{0:T(1024)S(1)} copy-done((s32[6144]{0:T(1024)S(1)}, s32[6144]{0:T(1024)}, u32[]{:S(2)}) %copy-start.4) | copy-done | bytes 24600
  4.6 0.0 copy-start.6
  4.6 0.7 %copy-done.6 = f32[12,64]{1,0:T(8,128)S(1)} copy-done((f32[12,64]{1,0:T(8,128)S(1)}, f32[12,64]{1,0:T(8,128)}, u32[]{:S(2)}) %copy-start.6) | copy-done | bytes 3096
  5.3 60.4 %shard_map.91 = f32[12,64]{1,0:T(8,128)S(1)} custom-call(bf16[192,512]{1,0:T(8,128)(2,1)S(1)} %bitcast.6, f32[12,64]{1,0:T(8,128)S(1)} %copy-done.5, f32[12,64]{1,0:T(8,128)S(1)} %copy-done.6, f32[1,64]{1,0:T(1,128)S(1)} %bitcast.11, s32[48,128]{1,0:T(8,128)S(1)} %bitcast.7, s32[48,128]{1,0:T(8,128)S(1)} %bitcast.8, s32[48,128]{1,0:T(8,128)S(1)} %bitcast.9, ...), custom_call_target="tpu_custom_call" | custom-call | tf_op jit(solution)/shard_map/pallas_call | solution.py:405
  65.7 0.6 copy.11
Async XLA Ops:
  0.0 0.7 %copy-start.5 = (f32[12,64]{1,0:T(8,128)S(1)}, f32[12,64]{1,0:T(8,128)}, u32[]{:S(2)}) copy-start(f32[12,64]{1,0:T(8,128)} %state_ref.1) | copy-start | bytes 9220
  0.0 0.7 %copy-start.7 = (f32[64]{0:T(128)S(1)}, f32[64]{0:T(128)}, u32[]{:S(2)}) copy-start(f32[64]{0:T(128)} %param.12) | copy-start | bytes 772
  0.0 0.7 %copy-start.8 = (s32[1,128]{1,0:T(1,128)S(1)}, s32[1,128]{1,0:T(1,128)}, u32[]{:S(2)}) copy-start(s32[1,128]{1,0:T(1,128)} %counts_ref.1) | copy-start | bytes 1540
  0.7 0.9 %copy-start = (bf16[3,64,512]{2,1,0:T(8,128)(2,1)S(1)}, bf16[3,64,512]{2,1,0:T(8,128)(2,1)}, u32[]{:S(2)}) copy-start(bf16[3,64,512]{2,1,0:T(8,128)(2,1)} %param.9) | copy-start | bytes 589828
  1.6 0.7 %copy-start.1 = (s32[6144]{0:T(1024)S(1)}, s32[6144]{0:T(1024)}, u32[]{:S(2)}) copy-start(s32[6144]{0:T(1024)} %param.13) | copy-start | bytes 73732
  2.4 0.7 %copy-start.2 = (s32[6144]{0:T(1024)S(1)}, s32[6144]{0:T(1024)}, u32[]{:S(2)}) copy-start(s32[6144]{0:T(1024)} %param.14) | copy-start | bytes 73732
  3.1 0.7 %copy-start.3 = (s32[6144]{0:T(1024)S(1)}, s32[6144]{0:T(1024)}, u32[]{:S(2)}) copy-start(s32[6144]{0:T(1024)} %param.15) | copy-start | bytes 73732
  3.8 0.7 %copy-start.4 = (s32[6144]{0:T(1024)S(1)}, s32[6144]{0:T(1024)}, u32[]{:S(2)}) copy-start(s32[6144]{0:T(1024)} %param.16) | copy-start | bytes 73732
  4.6 0.7 %copy-start.6 = (f32[12,64]{1,0:T(8,128)S(1)}, f32[12,64]{1,0:T(8,128)}, u32[]{:S(2)}) copy-start(f32[12,64]{1,0:T(8,128)} %pred_ref.1) | copy-start | bytes 9220

commit v2 on v1

--- a/solution.py
+++ b/solution.py
@@ -21,8 +21,8 @@
 NC = 8
 DENSE = (ROWS // 128, 128)
 PER_G = ROWS // NG
-W_NEAR = 512
-W_FAR = 256
+W = 256
+FEATURES = 88
 NT = (((1,), (1,)), ((), ()))
 
 MN = [(m, n) for m in range(4) for n in range(m, 4)]
@@ -38,6 +38,10 @@
     rows = (iota((V, width), 0) - V // 2).astype(BF16)
     mine = jnp.broadcast_to((vertex - V // 2).astype(BF16), (V, width))
     return jnp.where(rows == mine, jnp.ones((), BF16), jnp.zeros((), BF16))
+
+
+def pair_of(ref, j):
+    return jnp.concatenate([ref[pl.ds(2 * j, 1), :], ref[pl.ds(2 * j + 1, 1), :]], axis=1)
 
 
 def pick_bodies(acc, picked, body, blocks):
@@ -85,11 +89,12 @@
 
 
 def kernel(
-    rest_ref, state_ref, pred_ref, mass_ref, nb_ref, nv_ref, fb_ref, fv_ref, counts_ref,
+    rest_in, state_in, pred_in, mass_in, nb_in, nv_in, fb_in, fv_in, counts_in,
     out_ref,
+    state_ref, pred_ref, mass_ref, nb_ref, nv_ref, fb_ref, fv_ref, counts_ref,
     restg, ksend, krecv, ssend, srecv, xsend, xrecv,
-    oh, ohb, acc, keyd, vrow, brow, nbrow, nvrow, fbd, fr, nr, live, p16, q9, feat, tot, inert, xd,
-    rest_ss, rest_rs, k_ss, k_rs, s_ss, s_rs, x_ss, x_rs,
+    oh, ohb, acc, keyd, fkd, fr, nr, live, p16, q8, q2, feat, tot, inert, xd,
+    in_s, rest_ss, rest_rs, k_ss, k_rs, s_ss, s_rs, x_ss, x_rs,
 ):
     g = lax.axis_index("group")
     c = lax.axis_index("cell")
@@ -101,6 +106,19 @@
     def group_peer(d):
         return lax.rem(g + d, NG)
 
+    to_vmem = [
+        pltpu.make_async_copy(source, target, in_s.at[n])
+        for n, (source, target) in enumerate(
+            (
+                (fb_in, fb_ref), (fv_in, fv_ref), (state_in, state_ref), (nv_in, nv_ref),
+                (nb_in, nb_ref), (rest_in, restg.at[c]), (counts_in, counts_ref),
+                (mass_in, mass_ref), (pred_in, pred_ref),
+            )
+        )
+    ]
+    for copy in to_vmem:
+        copy.start()
+
     barrier = pltpu.get_barrier_semaphore()
 
     @pl.loop(1, NC)
@@ -110,6 +128,9 @@
     @pl.loop(1, NG)
     def _(d):
         pl.semaphore_signal(barrier, inc=1, device_id=(group_peer(d), c), device_id_type=MESH)
+
+    for copy in to_vmem[:3]:
+        copy.wait()
 
     for t in range(3):
         rows = pl.ds(t, NG, stride=3)
@@ -128,11 +149,31 @@
             device_id=(g, to), device_id_type=MESH,
         )
 
-    def rest_copy(to, slot):
+    x, core = lax.div(c, 2), lax.rem(c, 2)
+    chips = [lax.rem(x + d, NC // 2) for d in range(NC // 2)]
+    here, right, opposite, left = chips
+    other = here * 2 + 1 - core
+    halves = (pl.ds(0, 3 * B // 2), pl.ds(3 * B // 2, 3 * B // 2))
+
+    def rest_copy(n, slot, to, half=None):
+        ref = restg.at[slot] if half is None else restg.at[slot, halves[half]]
         return pltpu.make_async_remote_copy(
-            rest_ref, restg.at[slot], rest_ss.at[to], rest_rs.at[slot],
+            ref, ref, rest_ss.at[n], rest_rs.at[slot, half or 0],
             device_id=(g, to), device_id_type=MESH,
         )
+
+    rest_sends = [
+        pltpu.make_async_remote_copy(
+            rest_in, restg.at[c], rest_ss.at[n], rest_rs.at[c, 0],
+            device_id=(g, to), device_id_type=MESH,
+        )
+        for n, to in enumerate((other, right * 2 + core, left * 2 + core))
+    ]
+
+    def hand_on(n, slot, to, half=None):
+        copy = rest_copy(n, slot, to, half)
+        copy.start()
+        rest_sends.append(copy)
 
     def state_copy(it, to, slot):
         return pltpu.make_async_remote_copy(
@@ -150,45 +191,39 @@
     def _(d):
         key_copy(cell_peer(d), c).start()
 
+    for copy in rest_sends:
+        copy.start()
+
     @pl.loop(1, NC)
     def _(d):
-        rest_copy(cell_peer(d), c).start()
-
-    @pl.loop(1, NC)
-    def _(d):
         state_copy(0, cell_peer(d), c).start()
 
-    restg[c] = rest_ref[...]
     krecv[c] = ksend[c]
     srecv[0, c] = ssend[0]
-
-    @pl.loop(0, DENSE[0])
-    def _(j):
-        lanes = pl.ds(pl.multiple_of(j * 128, 128), 128)
-        nvrow[0:1, lanes] = nv_ref[pl.ds(j, 1), :]
-        nbrow[0:1, lanes] = nb_ref[pl.ds(j, 1), :]
+    for copy in to_vmem[3:]:
+        copy.wait()
 
     p16[...] = jnp.zeros_like(p16)
 
-    @pl.loop(0, ROWS // W_NEAR)
-    def _(j):
-        lanes = pl.ds(pl.multiple_of(j * W_NEAR, W_NEAR), W_NEAR)
-        picked = jnp.dot(
-            rest_ref[...], one_hot_vertex(nvrow[0:1, lanes]), preferred_element_type=F32
-        )
-        body = nbrow[0:1, lanes]
+    def near_lookup(j, carry):
+        lanes = pl.ds(pl.multiple_of(j * W, W), W)
+        picked = jnp.dot(restg[c], one_hot_vertex(pair_of(nv_ref, j)), preferred_element_type=F32)
+        body = pair_of(nb_ref, j)
         ohb[:, lanes] = jnp.where(
-            iota((B, W_NEAR), 0) == jnp.broadcast_to(body, (B, W_NEAR)), 1.0, 0.0
+            iota((B, W), 0) == jnp.broadcast_to(body, (B, W)), 1.0, 0.0
         ).astype(BF16)
-        tile = jnp.broadcast_to(body, (8, W_NEAR)) - iota((8, W_NEAR), 0)
-        found = pick_bodies([jnp.zeros((8, W_NEAR), F32)] * 3, picked, tile, 1)
+        tile = jnp.broadcast_to(body, (8, W)) - iota((8, W), 0)
+        found = pick_bodies([jnp.zeros((8, W), F32)] * 3, picked, tile, 1)
         r = [jnp.sum(f, 0, keepdims=True) for f in found]
-        lever = [jnp.ones((1, W_NEAR), F32)] + r
+        lever = [jnp.ones((1, W), F32)] + r
         for f, (m, n) in enumerate(MN):
             p16[f : f + 1, lanes] = lever[m] * lever[n]
         for i in range(3):
-            for t in range(W_NEAR // 128):
-                nr[i, pl.ds(j * (W_NEAR // 128) + t, 1), :] = r[i][:, t * 128 : (t + 1) * 128]
+            for t in range(2):
+                nr[i, pl.ds(2 * j + t, 1), :] = r[i][:, t * 128 : (t + 1) * 128]
+        return carry
+
+    lax.fori_loop(0, ROWS // W, near_lookup, 0, unroll=4)
 
     row = iota(DENSE, 0) * 128 + iota(DENSE, 1)
     sender = (row * 43691) >> 21
@@ -196,7 +231,7 @@
     live[...] = jnp.where(row - sender * CAP < count, 1.0, 0.0)
 
     ones = jnp.ones((8, V), BF16)
-    body_rest = [rest_ref[i * B : (i + 1) * B, :] for i in range(3)]
+    body_rest = [restg[c, i * B : (i + 1) * B, :] for i in range(3)]
     scale = mass_ref[...] * (1.0 / V)
     inert[0:1, :] = mass_ref[...]
     for f, (m, n) in enumerate(MN):
@@ -219,48 +254,55 @@
     for s in range(NC):
         keyd[:, s * CAP : (s + 1) * CAP] = krecv[s, :, 0:CAP]
     for t in range(3):
-        fbd[pl.ds(t, NG, stride=3), :] = keyd[:, t * 128 : (t + 1) * 128] >> 9
-
-    @pl.loop(0, NG)
-    def _(j):
-        lanes = pl.ds(pl.multiple_of(j * PER_G, 128), PER_G)
-        key = keyd[pl.ds(j, 1), :]
-        vrow[0:1, lanes] = key & (V - 1)
-        brow[0:1, lanes] = key >> 9
-
-    @pl.loop(0, ROWS // W_NEAR)
-    def _(j):
-        lanes = pl.ds(pl.multiple_of(j * W_NEAR, W_NEAR), W_NEAR)
-        oh[:, lanes] = one_hot_vertex(vrow[0:1, lanes])
-
-    acc[...] = jnp.zeros_like(acc)
-    x = lax.div(c, 2)
-    for step, d in enumerate((0, 1, 3, 2)):
-        chip = lax.rem(x + d, NC // 2)
-        if step == 0:
-            rest_copy(c, c + 1 - 2 * lax.rem(c, 2)).wait_recv()
-        else:
-            for k in range(2):
-                rest_copy(c, chip * 2 + k).wait_recv()
-
-        def look(j, carry, chip=chip):
-            lanes = pl.ds(pl.multiple_of(j * W_FAR, W_FAR), W_FAR)
-            table = restg[pl.ds(chip * 2, 2)].reshape(2 * 3 * B, V)
-            picked = jnp.dot(table, oh[:, lanes], preferred_element_type=F32)
-            body = jnp.broadcast_to(brow[0:1, lanes] - chip * 2 * B, (8, W_FAR))
-            found = [acc[i * 8 : i * 8 + 8, lanes] for i in range(3)]
-            found = pick_bodies(found, picked, body - iota((8, W_FAR), 0), 2)
+        fkd[pl.ds(t, NG, stride=3), :] = keyd[:, t * 128 : (t + 1) * 128]
+
+    def look(where, first, last, start, stop):
+        def step(j, carry):
+            lanes = pl.ds(pl.multiple_of(j * W, W), W)
+            key = pair_of(fkd, j)
+            if first:
+                hot = one_hot_vertex(key & (V - 1))
+                oh[:, lanes] = hot
+                found = [jnp.zeros((8, W), F32)] * 3
+            else:
+                hot = oh[:, lanes]
+                found = [acc[i * 8 : i * 8 + 8, lanes] for i in range(3)]
+            body = jnp.broadcast_to(key >> 9, (8, W)) - iota((8, W), 0)
+            for chip in where:
+                table = restg[pl.ds(chip * 2, 2)].reshape(2 * 3 * B, V)
+                picked = jnp.dot(table, hot, preferred_element_type=F32)
+                found = pick_bodies(found, picked, body - chip * (2 * B), 2)
             for i in range(3):
-                acc[i * 8 : i * 8 + 8, lanes] = found[i]
+                if last:
+                    r = jnp.sum(found[i], 0, keepdims=True)
+                    for t in range(2):
+                        fr[i, pl.ds(2 * j + t, 1), :] = r[:, t * 128 : (t + 1) * 128]
+                else:
+                    acc[i * 8 : i * 8 + 8, lanes] = found[i]
             return carry
 
-        lax.fori_loop(0, ROWS // W_FAR, look, 0, unroll=4)
-
-    @pl.loop(0, DENSE[0])
-    def _(j):
-        lanes = pl.ds(pl.multiple_of(j * 128, 128), 128)
-        for i in range(3):
-            fr[i, pl.ds(j, 1), :] = jnp.sum(acc[i * 8 : i * 8 + 8, lanes], 0, keepdims=True)
+        lax.fori_loop(start, stop, step, 0, unroll=4)
+
+    chunks = ROWS // W
+    rest_copy(0, other, other).wait_recv()
+    look((here,), True, False, 0, chunks // 2)
+    for n, (chip, half, to) in enumerate(((left, 0, right), (right, 1, left))):
+        slot = chip * 2 + core
+        rest_copy(0, slot, other).wait_recv()
+        hand_on(3 + 2 * n, slot, to * 2 + core, half)
+        hand_on(4 + 2 * n, slot, other)
+    look((here,), True, False, chunks // 2, chunks)
+    for chip in (left, right):
+        rest_copy(0, chip * 2 + 1 - core, other).wait_recv()
+    look((left, right), False, False, 0, chunks // 2)
+    for half in range(2):
+        slot = opposite * 2 + core
+        rest_copy(0, slot, other, half).wait_recv()
+        hand_on(7 + half, slot, other, half)
+    look((left, right), False, False, chunks // 2, chunks)
+    for half in range(2):
+        rest_copy(0, opposite * 2 + 1 - core, other, half).wait_recv()
+    look((opposite,), False, True, 0, chunks)
 
     state = [state_ref[e : e + 1, :] for e in range(12)]
     for it in range(NEWTON):
@@ -269,24 +311,23 @@
             state_copy(it, c, cell_peer(d)).wait_recv()
 
         pick = iota((16, 128), 1) < B
-        low = fbd[...] & 127
-        chip_of = fbd[...] >> 7
+        low = (fkd[...] >> 9) & 127
+        chip_of = fkd[...] >> 16
         far = [None] * 12
         for chip in range(NC // 2):
             table = jnp.where(pick, srecv[it, 2 * chip], srecv[it, 2 * chip + 1])
-            here = chip_of == chip
+            mine = chip_of == chip
             for e in range(12):
                 value = gather_lanes(table[e : e + 1], low)
-                far[e] = value if chip == 0 else jnp.where(here, value, far[e])
+                far[e] = value if chip == 0 else jnp.where(mine, value, far[e])
         for i in range(3):
             xd[i] = far[i] + fr[0] * far[3 + i] + fr[1] * far[6 + i] + fr[2] * far[9 + i]
 
-        @pl.loop(0, NG)
-        def _(j, it=it):
+        for j in range(NG):
             for i in range(3):
                 for t in range(3):
                     at = i * PER_G + t * 128
-                    xsend[it, j, :, at : at + 128] = xd[i, pl.ds(j * 3 + t, 1), :]
+                    xsend[it, j, :, at : at + 128] = xd[i, j * 3 + t : j * 3 + t + 1, :]
 
         @pl.loop(1, NG)
         def _(d, it=it):
@@ -305,12 +346,11 @@
         def _(d, it=it):
             x_copy(it, g, group_peer(d)).wait_recv()
 
-        @pl.loop(0, NG)
-        def _(j, it=it):
+        for j in range(NG):
             for i in range(3):
                 for t in range(3):
                     at = i * PER_G + t * 128
-                    xd[i, pl.ds(j * 3 + t, 1), :] = xrecv[it, j, :, at : at + 128]
+                    xd[i, j * 3 + t : j * 3 + t + 1, :] = xrecv[it, j, :, at : at + 128]
 
         off = [near_x[i] - xd[i] for i in range(3)]
         w = 1.0 / (off[0] * off[0] + off[1] * off[1] + off[2] * off[2] + 1.0)
@@ -318,33 +358,24 @@
         h2 = 4.0 * h1 * w
         for f, (i, k) in enumerate(IK):
             value = h2 * off[i] * off[k]
-            q9[f] = value + h1 if i == k else value
-        for i in range(3):
-            q9[6 + i] = -h1 * off[i]
+            q8[pl.ds(f, DENSE[0], stride=8), :] = value + h1 if i == k else value
+        for i in range(2):
+            q8[pl.ds(6 + i, DENSE[0], stride=8), :] = -h1 * off[i]
+        q2[...] = -h1 * off[2]
 
         def features(j, carry):
             lanes = pl.ds(pl.multiple_of(j * 128, 128), 128)
-            lever = p16[:, lanes]
-            for f in range(6):
-                value = lever * q9[f, pl.ds(j, 1), :]
-                high = value.astype(BF16)
-                feat[f * 16 : f * 16 + 16, lanes] = high
-                feat[128 + f * 16 : 128 + f * 16 + 16, lanes] = (value - high.astype(F32)).astype(
-                    BF16
-                )
-            for f, pair in enumerate(((6, 7), (8, 8))):
-                value = jnp.concatenate(
-                    [lever[0:8] * q9[q, pl.ds(j, 1), :] for q in pair], axis=0
-                )
-                high = value.astype(BF16)
-                at = 96 + f * 16
-                feat[at : at + 16, lanes] = high
-                feat[128 + at : 128 + at + 16, lanes] = (value - high.astype(F32)).astype(BF16)
+            terms = q8[pl.ds(pl.multiple_of(j * 8, 8), 8), :]
+            values = [terms * p16[f : f + 1, lanes] for f in range(10)]
+            values.append(p16[0:8, lanes] * q2[pl.ds(j, 1), :])
+            high = [value.astype(BF16) for value in values]
+            low = [(v - h.astype(F32)).astype(BF16) for v, h in zip(values, high)]
+            feat[:, lanes] = jnp.concatenate(high + low, axis=0)
             return carry
 
-        lax.fori_loop(0, DENSE[0], features, 0, unroll=2)
+        lax.fori_loop(0, DENSE[0], features, 0, unroll=4)
         both = lax.dot_general(feat[...], ohb[...], NT, preferred_element_type=F32)
-        tot[...] = both[0:128] + both[128:256]
+        tot[...] = both[0:FEATURES] + both[FEATURES : 2 * FEATURES]
 
         def moment(m, n):
             f = MN.index((min(m, n), max(m, n)))
@@ -352,7 +383,7 @@
 
         def hess(a, b):
             (m, i), (n, k) = divmod(a, 3), divmod(b, 3)
-            f = IK.index((min(i, k), max(i, k))) * 16 + MN.index((min(m, n), max(m, n)))
+            f = IK.index((min(i, k), max(i, k))) + MN.index((min(m, n), max(m, n))) * 8
             value = tot[f : f + 1, :]
             if i == k:
                 value = value + moment(m, n)
@@ -364,7 +395,7 @@
         grad = []
         for e in range(12):
             m, i = divmod(e, 3)
-            at = 96 + i * 8 + m
+            at = m * 8 + 6 + i if i < 2 else 80 + m
             value = tot[at : at + 1, :]
             for n in range(4):
                 value = value + moment(m, n) * shift[3 * n + i]
@@ -386,10 +417,12 @@
             for e in range(12):
                 out_ref[e : e + 1, :] = state[e]
 
+    for copy in rest_sends:
+        copy.wait_send()
+
     @pl.loop(1, NC)
     def _(d):
         key_copy(cell_peer(d), c).wait_send()
-        rest_copy(cell_peer(d), c).wait_send()
         for it in range(NEWTON):
             state_copy(it, cell_peer(d), c).wait_send()
 
@@ -405,9 +438,17 @@
     return pl.pallas_call(
         kernel,
         out_shape=jax.ShapeDtypeStruct((12, B), F32),
-        in_specs=[pl.BlockSpec(memory_space=vmem)] * 9,
+        in_specs=[pl.BlockSpec(memory_space=pltpu.HBM)] * 9,
         out_specs=pl.BlockSpec(memory_space=vmem),
         scratch_shapes=[
+            vmem((12, B), F32),
+            vmem((12, B), F32),
+            vmem((1, B), F32),
+            vmem(DENSE, I32),
+            vmem(DENSE, I32),
+            vmem(DENSE, I32),
+            vmem(DENSE, I32),
+            vmem((1, 128), I32),
             vmem((NC, 3 * B, V), BF16),
             vmem((NC, NG, 128), I32),
             vmem((NC, NG, 128), I32),
@@ -419,22 +460,20 @@
             vmem((B, ROWS), BF16),
             vmem((24, ROWS), F32),
             vmem((NG, PER_G), I32),
-            vmem((1, ROWS), I32),
-            vmem((1, ROWS), I32),
-            vmem((1, ROWS), I32),
-            vmem((1, ROWS), I32),
             vmem(DENSE, I32),
             vmem((3,) + DENSE, F32),
             vmem((3,) + DENSE, F32),
             vmem(DENSE, F32),
             vmem((16, ROWS), F32),
-            vmem((9,) + DENSE, F32),
-            vmem((256, ROWS), BF16),
-            vmem((128, B), F32),
+            vmem((8 * DENSE[0], 128), F32),
+            vmem(DENSE, F32),
+            vmem((2 * FEATURES, ROWS), BF16),
+            vmem((FEATURES, B), F32),
             vmem((16, B), F32),
             vmem((3,) + DENSE, F32),
-            dma((NC,)),
-            dma((NC,)),
+            dma((9,)),
+            dma((9,)),
+            dma((NC, 2)),
             dma((NC,)),
             dma((NC,)),
             dma((NEWTON, NC)),
@@ -443,7 +482,7 @@
             dma((NEWTON, NG)),
         ],
         compiler_params=pltpu.CompilerParams(
-            collective_id=0, has_side_effects=True, vmem_limit_bytes=48 * 2**20
+            collective_id=0, has_side_effects=True, vmem_limit_bytes=60 * 2**20
         ),
     )(
         rest.reshape(3 * B, V),

time: 66.8 us -> 50.5 us (0.76)
  Pallas kernels: 60.4 us -> 49.1 us
  local copies, waits for them, and re-layouts: 5.87 us -> 1.3 us
    pallas_call x1, Pallas kernels: 60.4 us -> 49.1 us  [on_device(): pl.pallas_call(kernel, out_shape=jax.ShapeDtypeStruct((12, B), F32), in_s...]
    unnamed x19 -> x1, local copies, waits for them, and re-layouts: 5.87 us -> 1.3 us
where the time goes in v2:
time: 50.5 us; the launch traced here: 50.4 us
  Pallas kernels  49.1 us (97%)
  local copies, waits for them, and re-layouts  1.3 us (3%)
    pallas_call x1, Pallas kernels, on_device(): pl.pallas_call(kernel, out_shape=jax.ShapeDtypeStruct((12, B), F32), in_s...  49.1 us
    unnamed x1, local copies, waits for them, and re-layouts  1.3 us

profile of v2, /device:TPU:1, one launch (start us, length us, event | category | flops | bytes accessed | tf_op | source)
XLA Modules:
  0.0 50.4 jit_solution(11132734241288615349)
XLA Ops:
  0.0 49.1 %shard_map.91 = f32[12,64]{1,0:T(8,128)} custom-call(bf16[192,512]{1,0:T(8,128)(2,1)} %bitcast.6, f32[12,64]{1,0:T(8,128)} %state_in.1, f32[12,64]{1,0:T(8,128)} %pred_in.1, f32[1,64]{1,0:T(1,128)} %bitcast.11, s32[48,128]{1,0:T(8,128)} %bitcast.7, s32[48,128]{1,0:T(8,128)} %bitcast.8, s32[48,128]{1,0:T(8,128)} %bitcast.9, s32[48,128]{1,0:T(8,128)} %bitcast.10, ...), custom_call_target="tpu_custom_call" | custom-call | tf_op jit(solution)/shard_map/pallas_call | solution.py:438
  49.1 1.3 %copy.11 = f32[12,64]{1,0:T(8,128)} copy(f32[12,64]{1,0:T(8,128)} %shard_map.91) | data formatting | bytes 6144

commit v3 on v2

--- a/solution.py
+++ b/solution.py
@@ -22,6 +22,11 @@
 DENSE = (ROWS // 128, 128)
 PER_G = ROWS // NG
 W = 256
+NEAREST = sorted(
+    ((z, y) for z in range(4) for y in range(4)),
+    key=lambda d: min(d[0], 4 - d[0]) + min(d[1], 4 - d[1]),
+)
+PART = 8
 FEATURES = 88
 NT = (((1,), (1,)), ((), ()))
 
@@ -93,7 +98,7 @@
     out_ref,
     state_ref, pred_ref, mass_ref, nb_ref, nv_ref, fb_ref, fv_ref, counts_ref,
     restg, ksend, krecv, ssend, srecv, xsend, xrecv,
-    oh, ohb, acc, keyd, fkd, fr, nr, live, p16, q8, q2, feat, tot, inert, xd,
+    oh, ohb, acc, keyd, fkd, fr, nr, nb, nv, live, p16, q8, q2, feat, tot, inert, xd,
     in_s, rest_ss, rest_rs, k_ss, k_rs, s_ss, s_rs, x_ss, x_rs,
 ):
     g = lax.axis_index("group")
@@ -102,6 +107,9 @@
 
     def cell_peer(d):
         return lax.rem(c + d, NC)
+
+    z, y = lax.div(g, 4), lax.rem(g, 4)
+    groups = [lax.rem(z + dz, 4) * 4 + lax.rem(y + dy, 4) for dz, dy in NEAREST]
 
     def group_peer(d):
         return lax.rem(g + d, NG)
@@ -203,12 +211,25 @@
     for copy in to_vmem[3:]:
         copy.wait()
 
+    row = iota(DENSE, 0) * 128 + iota(DENSE, 1)
+    sender = (row * 43691) >> 21
+    count = gather_lanes(counts_ref[...], sender)
+    xd[0] = jnp.where(row - sender * CAP < count, 1.0, 0.0)
+
+    for q, group in enumerate(groups):
+        for t in range(3):
+            at = pl.ds(group * 3 + t, 1)
+            to = pl.ds(q * 3 + t, 1)
+            nb[to, :] = nb_ref[at, :]
+            nv[to, :] = nv_ref[at, :]
+            live[to, :] = xd[0, at, :]
+
     p16[...] = jnp.zeros_like(p16)
 
     def near_lookup(j, carry):
         lanes = pl.ds(pl.multiple_of(j * W, W), W)
-        picked = jnp.dot(restg[c], one_hot_vertex(pair_of(nv_ref, j)), preferred_element_type=F32)
-        body = pair_of(nb_ref, j)
+        picked = jnp.dot(restg[c], one_hot_vertex(pair_of(nv, j)), preferred_element_type=F32)
+        body = pair_of(nb, j)
         ohb[:, lanes] = jnp.where(
             iota((B, W), 0) == jnp.broadcast_to(body, (B, W)), 1.0, 0.0
         ).astype(BF16)
@@ -224,11 +245,6 @@
         return carry
 
     lax.fori_loop(0, ROWS // W, near_lookup, 0, unroll=4)
-
-    row = iota(DENSE, 0) * 128 + iota(DENSE, 1)
-    sender = (row * 43691) >> 21
-    count = gather_lanes(counts_ref[...], sender)
-    live[...] = jnp.where(row - sender * CAP < count, 1.0, 0.0)
 
     ones = jnp.ones((8, V), BF16)
     body_rest = [restg[c, i * B : (i + 1) * B, :] for i in range(3)]
@@ -335,46 +351,49 @@
 
         xrecv[it, g] = xsend[it, g]
 
-        near_index = nb_ref[...]
+        near_index = nb[...]
         near = [gather_lanes(jnp.concatenate([s, s], axis=1), near_index) for s in state]
         near_x = [
             near[i] + nr[0] * near[3 + i] + nr[1] * near[6 + i] + nr[2] * near[9 + i]
             for i in range(3)
         ]
 
-        @pl.loop(1, NG)
-        def _(d, it=it):
-            x_copy(it, g, group_peer(d)).wait_recv()
-
-        for j in range(NG):
-            for i in range(3):
-                for t in range(3):
-                    at = i * PER_G + t * 128
-                    xd[i, j * 3 + t : j * 3 + t + 1, :] = xrecv[it, j, :, at : at + 128]
-
-        off = [near_x[i] - xd[i] for i in range(3)]
-        w = 1.0 / (off[0] * off[0] + off[1] * off[1] + off[2] * off[2] + 1.0)
-        h1 = (2.0 * kc) * w * w * live[...]
-        h2 = 4.0 * h1 * w
-        for f, (i, k) in enumerate(IK):
-            value = h2 * off[i] * off[k]
-            q8[pl.ds(f, DENSE[0], stride=8), :] = value + h1 if i == k else value
-        for i in range(2):
-            q8[pl.ds(6 + i, DENSE[0], stride=8), :] = -h1 * off[i]
-        q2[...] = -h1 * off[2]
-
-        def features(j, carry):
-            lanes = pl.ds(pl.multiple_of(j * 128, 128), 128)
-            terms = q8[pl.ds(pl.multiple_of(j * 8, 8), 8), :]
-            values = [terms * p16[f : f + 1, lanes] for f in range(10)]
-            values.append(p16[0:8, lanes] * q2[pl.ds(j, 1), :])
-            high = [value.astype(BF16) for value in values]
-            low = [(v - h.astype(F32)).astype(BF16) for v, h in zip(values, high)]
-            feat[:, lanes] = jnp.concatenate(high + low, axis=0)
-            return carry
-
-        lax.fori_loop(0, DENSE[0], features, 0, unroll=4)
-        both = lax.dot_general(feat[...], ohb[...], NT, preferred_element_type=F32)
+        both = jnp.zeros((2 * FEATURES, B), F32)
+        for part in range(0, NG, PART):
+            for q in range(part, part + PART):
+                if q:
+                    x_copy(it, g, groups[q]).wait_recv()
+                for i in range(3):
+                    for t in range(3):
+                        at = i * PER_G + t * 128
+                        xd[i, q * 3 + t : q * 3 + t + 1, :] = xrecv[it, groups[q], :, at : at + 128]
+
+            rows = slice(part * 3, (part + PART) * 3)
+            off = [near_x[i][rows] - xd[i, rows] for i in range(3)]
+            w = 1.0 / (off[0] * off[0] + off[1] * off[1] + off[2] * off[2] + 1.0)
+            h1 = (2.0 * kc) * w * w * live[rows]
+            h2 = 4.0 * h1 * w
+            for f, (i, k) in enumerate(IK):
+                value = h2 * off[i] * off[k]
+                at = pl.ds(rows.start * 8 + f, PART * 3, stride=8)
+                q8[at, :] = value + h1 if i == k else value
+            for i in range(2):
+                q8[pl.ds(rows.start * 8 + 6 + i, PART * 3, stride=8), :] = -h1 * off[i]
+            q2[rows, :] = -h1 * off[2]
+
+            for first in range(rows.start, rows.stop, 8):
+                for j in range(first, first + 8):
+                    lanes = pl.ds(j * 128, 128)
+                    terms = q8[j * 8 : j * 8 + 8, :]
+                    values = [terms * p16[f : f + 1, lanes] for f in range(10)]
+                    values.append(p16[0:8, lanes] * q2[j : j + 1, :])
+                    high = [value.astype(BF16) for value in values]
+                    low = [(v - h.astype(F32)).astype(BF16) for v, h in zip(values, high)]
+                    feat[:, lanes] = jnp.concatenate(high + low, axis=0)
+                block = pl.ds(first * 128, 8 * 128)
+                both = both + lax.dot_general(
+                    feat[:, block], ohb[:, block], NT, preferred_element_type=F32
+                )
         tot[...] = both[0:FEATURES] + both[FEATURES : 2 * FEATURES]
 
         def moment(m, n):
@@ -463,6 +482,8 @@
             vmem(DENSE, I32),
             vmem((3,) + DENSE, F32),
             vmem((3,) + DENSE, F32),
+            vmem(DENSE, I32),
+            vmem(DENSE, I32),
             vmem(DENSE, F32),
             vmem((16, ROWS), F32),
             vmem((8 * DENSE[0], 128), F32),

time: 50.5 us -> 47.7 us (0.945)
  Pallas kernels: 49.1 us -> 46.3 us
    pallas_call x1, Pallas kernels: 49.1 us -> 46.3 us  [on_device(): pl.pallas_call(kernel, out_shape=jax.ShapeDtypeStruct((12, B), F32), in_s...]
where the time goes in v3:
time: 47.7 us; the launch traced here: 47.6 us
  Pallas kernels  46.3 us (97%)
  local copies, waits for them, and re-layouts  1.3 us (3%)
    pallas_call x1, Pallas kernels, on_device(): pl.pallas_call(kernel, out_shape=jax.ShapeDtypeStruct((12, B), F32), in_s...  46.3 us
    unnamed x1, local copies, waits for them, and re-layouts  1.3 us

profile of v3, /device:TPU:1, one launch (start us, length us, event | category | flops | bytes accessed | tf_op | source)
XLA Modules:
  0.0 47.6 jit_solution(2676244789300070386)
XLA Ops:
  0.0 46.3 %shard_map.91 = f32[12,64]{1,0:T(8,128)} custom-call(bf16[192,512]{1,0:T(8,128)(2,1)} %bitcast.6, f32[12,64]{1,0:T(8,128)} %state_in.1, f32[12,64]{1,0:T(8,128)} %pred_in.1, f32[1,64]{1,0:T(1,128)} %bitcast.11, s32[48,128]{1,0:T(8,128)} %bitcast.7, s32[48,128]{1,0:T(8,128)} %bitcast.8, s32[48,128]{1,0:T(8,128)} %bitcast.9, s32[48,128]{1,0:T(8,128)} %bitcast.10, ...), custom_call_target="tpu_custom_call" | custom-call | tf_op jit(solution)/shard_map/pallas_call | solution.py:457
  46.3 1.3 %copy.11 = f32[12,64]{1,0:T(8,128)} copy(f32[12,64]{1,0:T(8,128)} %shard_map.91) | data formatting | bytes 6144

commit v4 on v3

--- a/solution.py
+++ b/solution.py
@@ -170,12 +170,20 @@
             device_id=(g, to), device_id_type=MESH,
         )
 
-    rest_sends = [
-        pltpu.make_async_remote_copy(
-            rest_in, restg.at[c], rest_ss.at[n], rest_rs.at[c, 0],
+    def first_copy(n, to, half=None):
+        source = rest_in if half is None else rest_in.at[halves[half]]
+        target = restg.at[c] if half is None else restg.at[c, halves[half]]
+        return pltpu.make_async_remote_copy(
+            source, target, rest_ss.at[n], rest_rs.at[c, half or 0],
             device_id=(g, to), device_id_type=MESH,
         )
-        for n, to in enumerate((other, right * 2 + core, left * 2 + core))
+
+    rest_sends = [
+        first_copy(0, right * 2 + core, 0),
+        first_copy(1, left * 2 + core, 1),
+        first_copy(2, other),
+        first_copy(3, right * 2 + core, 1),
+        first_copy(4, left * 2 + core, 0),
     ]
 
     def hand_on(n, slot, to, half=None):
@@ -284,10 +292,9 @@
                 hot = oh[:, lanes]
                 found = [acc[i * 8 : i * 8 + 8, lanes] for i in range(3)]
             body = jnp.broadcast_to(key >> 9, (8, W)) - iota((8, W), 0)
-            for chip in where:
-                table = restg[pl.ds(chip * 2, 2)].reshape(2 * 3 * B, V)
-                picked = jnp.dot(table, hot, preferred_element_type=F32)
-                found = pick_bodies(found, picked, body - chip * (2 * B), 2)
+            for slot in where:
+                picked = jnp.dot(restg[slot], hot, preferred_element_type=F32)
+                found = pick_bodies(found, picked, body - slot * B, 1)
             for i in range(3):
                 if last:
                     r = jnp.sum(found[i], 0, keepdims=True)
@@ -297,28 +304,29 @@
                     acc[i * 8 : i * 8 + 8, lanes] = found[i]
             return carry
 
-        lax.fori_loop(start, stop, step, 0, unroll=4)
+        lax.fori_loop(start, stop, step, 0, unroll=True)
 
     chunks = ROWS // W
     rest_copy(0, other, other).wait_recv()
-    look((here,), True, False, 0, chunks // 2)
+    look((c, other), True, False, 0, 10)
     for n, (chip, half, to) in enumerate(((left, 0, right), (right, 1, left))):
-        slot = chip * 2 + core
-        rest_copy(0, slot, other).wait_recv()
-        hand_on(3 + 2 * n, slot, to * 2 + core, half)
-        hand_on(4 + 2 * n, slot, other)
-    look((here,), True, False, chunks // 2, chunks)
-    for chip in (left, right):
-        rest_copy(0, chip * 2 + 1 - core, other).wait_recv()
-    look((left, right), False, False, 0, chunks // 2)
+        rest_copy(0, chip * 2 + core, other, half).wait_recv()
+        hand_on(5 + n, chip * 2 + core, to * 2 + core, half)
+    look((c, other), True, False, 10, 24)
+    for n, (chip, half) in enumerate(((left, 1), (right, 0))):
+        rest_copy(0, chip * 2 + core, other, half).wait_recv()
+        hand_on(7 + n, chip * 2 + core, other)
+    look((left * 2 + core, right * 2 + core), False, False, 0, 24)
     for half in range(2):
         slot = opposite * 2 + core
         rest_copy(0, slot, other, half).wait_recv()
-        hand_on(7 + half, slot, other, half)
-    look((left, right), False, False, chunks // 2, chunks)
+        hand_on(9 + half, slot, other, half)
+    for chip in (left, right):
+        rest_copy(0, chip * 2 + 1 - core, other).wait_recv()
+    look((left * 2 + 1 - core, right * 2 + 1 - core), False, False, 0, chunks)
     for half in range(2):
         rest_copy(0, opposite * 2 + 1 - core, other, half).wait_recv()
-    look((opposite,), False, True, 0, chunks)
+    look((opposite * 2 + core, opposite * 2 + 1 - core), False, True, 0, chunks)
 
     state = [state_ref[e : e + 1, :] for e in range(12)]
     for it in range(NEWTON):
@@ -493,7 +501,7 @@
             vmem((16, B), F32),
             vmem((3,) + DENSE, F32),
             dma((9,)),
-            dma((9,)),
+            dma((11,)),
             dma((NC, 2)),
             dma((NC,)),
             dma((NC,)),

time: 47.7 us -> 44.4 us (0.931)
  Pallas kernels: 46.3 us -> 43 us
    pallas_call x1, Pallas kernels: 46.3 us -> 43 us  [on_device(): pl.pallas_call(kernel, out_shape=jax.ShapeDtypeStruct((12, B), F32), in_s...]
where the time goes in v4:
time: 44.4 us; the launch traced here: 44.3 us
  Pallas kernels  43 us (97%)
  local copies, waits for them, and re-layouts  1.3 us (3%)
    pallas_call x1, Pallas kernels, on_device(): pl.pallas_call(kernel, out_shape=jax.ShapeDtypeStruct((12, B), F32), in_s...  43 us
    unnamed x1, local copies, waits for them, and re-layouts  1.3 us

profile of v4, /device:TPU:1, one launch (start us, length us, event | category | flops | bytes accessed | tf_op | source)
XLA Modules:
  0.0 44.3 jit_solution(10584465170055241475)
XLA Ops:
  0.0 43.0 %shard_map.91 = f32[12,64]{1,0:T(8,128)} custom-call(bf16[192,512]{1,0:T(8,128)(2,1)} %bitcast.6, f32[12,64]{1,0:T(8,128)} %state_in.1, f32[12,64]{1,0:T(8,128)} %pred_in.1, f32[1,64]{1,0:T(1,128)} %bitcast.11, s32[48,128]{1,0:T(8,128)} %bitcast.7, s32[48,128]{1,0:T(8,128)} %bitcast.8, s32[48,128]{1,0:T(8,128)} %bitcast.9, s32[48,128]{1,0:T(8,128)} %bitcast.10, ...), custom_call_target="tpu_custom_call" | custom-call | tf_op jit(solution)/shard_map/pallas_call | solution.py:465
  43.0 1.3 %copy.11 = f32[12,64]{1,0:T(8,128)} copy(f32[12,64]{1,0:T(8,128)} %shard_map.91) | data formatting | bytes 6144

commit v5 on v4

--- a/solution.py
+++ b/solution.py
@@ -26,7 +26,7 @@
     ((z, y) for z in range(4) for y in range(4)),
     key=lambda d: min(d[0], 4 - d[0]) + min(d[1], 4 - d[1]),
 )
-PART = 8
+PART = 4
 FEATURES = 88
 NT = (((1,), (1,)), ((), ()))
 
@@ -98,7 +98,7 @@
     out_ref,
     state_ref, pred_ref, mass_ref, nb_ref, nv_ref, fb_ref, fv_ref, counts_ref,
     restg, ksend, krecv, ssend, srecv, xsend, xrecv,
-    oh, ohb, acc, keyd, fkd, fr, nr, nb, nv, live, p16, q8, q2, feat, tot, inert, xd,
+    oh, ohb, acc, keyd, fkd, fr, nr, nr4, nb, nv, live, p16, q8, q2, feat, tot, inert, xd,
     in_s, rest_ss, rest_rs, k_ss, k_rs, s_ss, s_rs, x_ss, x_rs,
 ):
     g = lax.axis_index("group")
@@ -129,12 +129,10 @@
 
     barrier = pltpu.get_barrier_semaphore()
 
-    @pl.loop(1, NC)
-    def _(d):
+    for d in range(1, NC):
         pl.semaphore_signal(barrier, inc=1, device_id=(g, cell_peer(d)), device_id_type=MESH)
 
-    @pl.loop(1, NG)
-    def _(d):
+    for d in range(1, NG):
         pl.semaphore_signal(barrier, inc=1, device_id=(group_peer(d), c), device_id_type=MESH)
 
     for copy in to_vmem[:3]:
@@ -203,15 +201,13 @@
             device_id=(to, c), device_id_type=MESH,
         )
 
-    @pl.loop(1, NC)
-    def _(d):
+    for d in range(1, NC):
         key_copy(cell_peer(d), c).start()
 
     for copy in rest_sends:
         copy.start()
 
-    @pl.loop(1, NC)
-    def _(d):
+    for d in range(1, NC):
         state_copy(0, cell_peer(d), c).start()
 
     krecv[c] = ksend[c]
@@ -271,8 +267,7 @@
             total = total + lax.dot_general(ones, low, NT, preferred_element_type=F32)
         inert[f : f + 1, :] = total[0:1] * scale
 
-    @pl.loop(1, NC)
-    def _(d):
+    for d in range(1, NC):
         key_copy(c, cell_peer(d)).wait_recv()
 
     for s in range(NC):
@@ -330,20 +325,21 @@
 
     state = [state_ref[e : e + 1, :] for e in range(12)]
     for it in range(NEWTON):
-        @pl.loop(1, NC)
-        def _(d, it=it):
-            state_copy(it, c, cell_peer(d)).wait_recv()
-
         pick = iota((16, 128), 1) < B
         low = (fkd[...] >> 9) & 127
         chip_of = fkd[...] >> 16
         far = [None] * 12
-        for chip in range(NC // 2):
+        for n, chip in enumerate((here, right, left, opposite)):
+            for k in range(2):
+                if n:
+                    state_copy(it, c, chip * 2 + k).wait_recv()
+                elif k:
+                    state_copy(it, c, other).wait_recv()
             table = jnp.where(pick, srecv[it, 2 * chip], srecv[it, 2 * chip + 1])
             mine = chip_of == chip
             for e in range(12):
                 value = gather_lanes(table[e : e + 1], low)
-                far[e] = value if chip == 0 else jnp.where(mine, value, far[e])
+                far[e] = value if n == 0 else jnp.where(mine, value, far[e])
         for i in range(3):
             xd[i] = far[i] + fr[0] * far[3 + i] + fr[1] * far[6 + i] + fr[2] * far[9 + i]
 
@@ -353,8 +349,7 @@
                     at = i * PER_G + t * 128
                     xsend[it, j, :, at : at + 128] = xd[i, j * 3 + t : j * 3 + t + 1, :]
 
-        @pl.loop(1, NG)
-        def _(d, it=it):
+        for d in range(1, NG):
             x_copy(it, group_peer(d), g).start()
 
         xrecv[it, g] = xsend[it, g]
@@ -366,6 +361,8 @@
             for i in range(3)
         ]
 
+        for i in range(3):
+            nr4[i] = near_x[i]
         both = jnp.zeros((2 * FEATURES, B), F32)
         for part in range(0, NG, PART):
             for q in range(part, part + PART):
@@ -377,7 +374,7 @@
                         xd[i, q * 3 + t : q * 3 + t + 1, :] = xrecv[it, groups[q], :, at : at + 128]
 
             rows = slice(part * 3, (part + PART) * 3)
-            off = [near_x[i][rows] - xd[i, rows] for i in range(3)]
+            off = [nr4[i, rows] - xd[i, rows] for i in range(3)]
             w = 1.0 / (off[0] * off[0] + off[1] * off[1] + off[2] * off[2] + 1.0)
             h1 = (2.0 * kc) * w * w * live[rows]
             h2 = 4.0 * h1 * w
@@ -389,8 +386,8 @@
                 q8[pl.ds(rows.start * 8 + 6 + i, PART * 3, stride=8), :] = -h1 * off[i]
             q2[rows, :] = -h1 * off[2]
 
-            for first in range(rows.start, rows.stop, 8):
-                for j in range(first, first + 8):
+            for first in range(rows.start, rows.stop, 4):
+                for j in range(first, first + 4):
                     lanes = pl.ds(j * 128, 128)
                     terms = q8[j * 8 : j * 8 + 8, :]
                     values = [terms * p16[f : f + 1, lanes] for f in range(10)]
@@ -398,7 +395,7 @@
                     high = [value.astype(BF16) for value in values]
                     low = [(v - h.astype(F32)).astype(BF16) for v, h in zip(values, high)]
                     feat[:, lanes] = jnp.concatenate(high + low, axis=0)
-                block = pl.ds(first * 128, 8 * 128)
+                block = pl.ds(first * 128, 4 * 128)
                 both = both + lax.dot_general(
                     feat[:, block], ohb[:, block], NT, preferred_element_type=F32
                 )
@@ -435,8 +432,7 @@
             for e in range(12):
                 ssend[it + 1, e : e + 1, :] = jnp.concatenate([state[e], state[e]], axis=1)
 
-            @pl.loop(1, NC)
-            def _(d, it=it):
+            for d in range(1, NC):
                 state_copy(it + 1, cell_peer(d), c).start()
 
             srecv[it + 1, c] = ssend[it + 1]
@@ -447,14 +443,12 @@
     for copy in rest_sends:
         copy.wait_send()
 
-    @pl.loop(1, NC)
-    def _(d):
+    for d in range(1, NC):
         key_copy(cell_peer(d), c).wait_send()
         for it in range(NEWTON):
             state_copy(it, cell_peer(d), c).wait_send()
 
-    @pl.loop(1, NG)
-    def _(d):
+    for d in range(1, NG):
         for it in range(NEWTON):
             x_copy(it, group_peer(d), g).wait_send()
 
@@ -488,6 +482,7 @@
             vmem((24, ROWS), F32),
             vmem((NG, PER_G), I32),
             vmem(DENSE, I32),
+            vmem((3,) + DENSE, F32),
             vmem((3,) + DENSE, F32),
             vmem((3,) + DENSE, F32),
             vmem(DENSE, I32),

time: 44.4 us -> 43.4 us (0.977)
  Pallas kernels: 43 us -> 41.9 us
    pallas_call x1, Pallas kernels: 43 us -> 41.9 us  [on_device(): pl.pallas_call(kernel, out_shape=jax.ShapeDtypeStruct((12, B), F32), in_s...]
where the time goes in v5:
time: 43.4 us; the launch traced here: 43.2 us
  Pallas kernels  41.9 us (97%)
  local copies, waits for them, and re-layouts  1.3 us (3%)
    pallas_call x1, Pallas kernels, on_device(): pl.pallas_call(kernel, out_shape=jax.ShapeDtypeStruct((12, B), F32), in_s...  41.9 us
    unnamed x1, local copies, waits for them, and re-layouts  1.3 us

profile of v5, /device:TPU:1, one launch (start us, length us, event | category | flops | bytes accessed | tf_op | source)
XLA Modules:
  0.0 43.2 jit_solution(1625084917572358114)
XLA Ops:
  0.0 41.9 %shard_map.91 = f32[12,64]{1,0:T(8,128)} custom-call(bf16[192,512]{1,0:T(8,128)(2,1)} %bitcast.6, f32[12,64]{1,0:T(8,128)} %state_in.1, f32[12,64]{1,0:T(8,128)} %pred_in.1, f32[1,64]{1,0:T(1,128)} %bitcast.11, s32[48,128]{1,0:T(8,128)} %bitcast.7, s32[48,128]{1,0:T(8,128)} %bitcast.8, s32[48,128]{1,0:T(8,128)} %bitcast.9, s32[48,128]{1,0:T(8,128)} %bitcast.10, ...), custom_call_target="tpu_custom_call" | custom-call | tf_op jit(solution)/shard_map/pallas_call | solution.py:459
  41.9 1.3 %copy.11 = f32[12,64]{1,0:T(8,128)} copy(f32[12,64]{1,0:T(8,128)} %shard_map.91) | data formatting | bytes 6144

commit v6 on v5

--- a/solution.py
+++ b/solution.py
@@ -26,7 +26,7 @@
     ((z, y) for z in range(4) for y in range(4)),
     key=lambda d: min(d[0], 4 - d[0]) + min(d[1], 4 - d[1]),
 )
-PART = 4
+PART = 2
 FEATURES = 88
 NT = (((1,), (1,)), ((), ()))
 
@@ -98,7 +98,7 @@
     out_ref,
     state_ref, pred_ref, mass_ref, nb_ref, nv_ref, fb_ref, fv_ref, counts_ref,
     restg, ksend, krecv, ssend, srecv, xsend, xrecv,
-    oh, ohb, acc, keyd, fkd, fr, nr, nr4, nb, nv, live, p16, q8, q2, feat, tot, inert, xd,
+    oh, ohb, acc, keyd, fkd, fr, early, nr, nr4, nb, nv, live, p16, q8, q2, feat, tot, inert, xd,
     in_s, rest_ss, rest_rs, k_ss, k_rs, s_ss, s_rs, x_ss, x_rs,
 ):
     g = lax.axis_index("group")
@@ -274,6 +274,24 @@
         keyd[:, s * CAP : (s + 1) * CAP] = krecv[s, :, 0:CAP]
     for t in range(3):
         fkd[pl.ds(t, NG, stride=3), :] = keyd[:, t * 128 : (t + 1) * 128]
+
+    def far_states(it):
+        pick = iota((16, 128), 1) < B
+        low = (fkd[...] >> 9) & 127
+        chip_of = fkd[...] >> 16
+        far = [None] * 12
+        for n, chip in enumerate((here, right, left, opposite)):
+            for k in range(2):
+                if n:
+                    state_copy(it, c, chip * 2 + k).wait_recv()
+                elif k:
+                    state_copy(it, c, other).wait_recv()
+            table = jnp.where(pick, srecv[it, 2 * chip], srecv[it, 2 * chip + 1])
+            mine = chip_of == chip
+            for e in range(12):
+                value = gather_lanes(table[e : e + 1], low)
+                far[e] = value if n == 0 else jnp.where(mine, value, far[e])
+        return far
 
     def look(where, first, last, start, stop):
         def step(j, carry):
@@ -319,27 +337,15 @@
     for chip in (left, right):
         rest_copy(0, chip * 2 + 1 - core, other).wait_recv()
     look((left * 2 + 1 - core, right * 2 + 1 - core), False, False, 0, chunks)
+    for e, value in enumerate(far_states(0)):
+        early[e] = value
     for half in range(2):
         rest_copy(0, opposite * 2 + 1 - core, other, half).wait_recv()
     look((opposite * 2 + core, opposite * 2 + 1 - core), False, True, 0, chunks)
 
     state = [state_ref[e : e + 1, :] for e in range(12)]
     for it in range(NEWTON):
-        pick = iota((16, 128), 1) < B
-        low = (fkd[...] >> 9) & 127
-        chip_of = fkd[...] >> 16
-        far = [None] * 12
-        for n, chip in enumerate((here, right, left, opposite)):
-            for k in range(2):
-                if n:
-                    state_copy(it, c, chip * 2 + k).wait_recv()
-                elif k:
-                    state_copy(it, c, other).wait_recv()
-            table = jnp.where(pick, srecv[it, 2 * chip], srecv[it, 2 * chip + 1])
-            mine = chip_of == chip
-            for e in range(12):
-                value = gather_lanes(table[e : e + 1], low)
-                far[e] = value if n == 0 else jnp.where(mine, value, far[e])
+        far = early if it == 0 else far_states(it)
         for i in range(3):
             xd[i] = far[i] + fr[0] * far[3 + i] + fr[1] * far[6 + i] + fr[2] * far[9 + i]
 
@@ -363,6 +369,17 @@
 
         for i in range(3):
             nr4[i] = near_x[i]
+        if it + 1 == NEWTON:
+            for copy in rest_sends:
+                copy.wait_send()
+            for d in range(1, NC):
+                key_copy(cell_peer(d), c).wait_send()
+                for n in range(NEWTON):
+                    state_copy(n, cell_peer(d), c).wait_send()
+            for n in range(NEWTON):
+                for d in range(1, NG):
+                    x_copy(n, group_peer(d), g).wait_send()
+
         both = jnp.zeros((2 * FEATURES, B), F32)
         for part in range(0, NG, PART):
             for q in range(part, part + PART):
@@ -386,8 +403,8 @@
                 q8[pl.ds(rows.start * 8 + 6 + i, PART * 3, stride=8), :] = -h1 * off[i]
             q2[rows, :] = -h1 * off[2]
 
-            for first in range(rows.start, rows.stop, 4):
-                for j in range(first, first + 4):
+            for first in range(rows.start, rows.stop, 6):
+                for j in range(first, first + 6):
                     lanes = pl.ds(j * 128, 128)
                     terms = q8[j * 8 : j * 8 + 8, :]
                     values = [terms * p16[f : f + 1, lanes] for f in range(10)]
@@ -395,7 +412,7 @@
                     high = [value.astype(BF16) for value in values]
                     low = [(v - h.astype(F32)).astype(BF16) for v, h in zip(values, high)]
                     feat[:, lanes] = jnp.concatenate(high + low, axis=0)
-                block = pl.ds(first * 128, 4 * 128)
+                block = pl.ds(first * 128, 6 * 128)
                 both = both + lax.dot_general(
                     feat[:, block], ohb[:, block], NT, preferred_element_type=F32
                 )
@@ -440,18 +457,6 @@
             for e in range(12):
                 out_ref[e : e + 1, :] = state[e]
 
-    for copy in rest_sends:
-        copy.wait_send()
-
-    for d in range(1, NC):
-        key_copy(cell_peer(d), c).wait_send()
-        for it in range(NEWTON):
-            state_copy(it, cell_peer(d), c).wait_send()
-
-    for d in range(1, NG):
-        for it in range(NEWTON):
-            x_copy(it, group_peer(d), g).wait_send()
-
 
 def on_device(rest, state, pred, mass, pair_body, pair_vertex, far_body, far_vertex, counts):
     dma = pltpu.SemaphoreType.DMA
@@ -483,6 +488,7 @@
             vmem((NG, PER_G), I32),
             vmem(DENSE, I32),
             vmem((3,) + DENSE, F32),
+            vmem((12,) + DENSE, F32),
             vmem((3,) + DENSE, F32),
             vmem((3,) + DENSE, F32),
             vmem(DENSE, I32),

time: 43.4 us -> 43.2 us (level)
  no operation moved by 1% of the time
where the time goes in v6:
time: 43.2 us; the launch traced here: 43.1 us
  Pallas kernels  41.7 us (97%)
  local copies, waits for them, and re-layouts  1.3 us (3%)
    pallas_call x1, Pallas kernels, on_device(): pl.pallas_call(kernel, out_shape=jax.ShapeDtypeStruct((12, B), F32), in_s...  41.7 us
    unnamed x1, local copies, waits for them, and re-layouts  1.3 us

profile of v6, /device:TPU:1, one launch (start us, length us, event | category | flops | bytes accessed | tf_op | source)
XLA Modules:
  0.0 43.1 jit_solution(1576708708887314393)
XLA Ops:
  0.0 41.7 %shard_map.91 = f32[12,64]{1,0:T(8,128)} custom-call(bf16[192,512]{1,0:T(8,128)(2,1)} %bitcast.6, f32[12,64]{1,0:T(8,128)} %state_in.1, f32[12,64]{1,0:T(8,128)} %pred_in.1, f32[1,64]{1,0:T(1,128)} %bitcast.11, s32[48,128]{1,0:T(8,128)} %bitcast.7, s32[48,128]{1,0:T(8,128)} %bitcast.8, s32[48,128]{1,0:T(8,128)} %bitcast.9, s32[48,128]{1,0:T(8,128)} %bitcast.10, ...), custom_call_target="tpu_custom_call" | custom-call | tf_op jit(solution)/shard_map/pallas_call | solution.py:464
  41.8 1.3 %copy.11 = f32[12,64]{1,0:T(8,128)} copy(f32[12,64]{1,0:T(8,128)} %shard_map.91) | data formatting | bytes 6144
